TPU v7x, 32 devices: a whole 2x2x4 slice. The times are simulated.
32 devices in a mesh: grp: 4 (over y, core), tile: 8 (over z, x).
Axes of the slice: x: 2, y: 2, z: 4, core: 2. Of those that a mesh axis runs over, the one named last changes fastest.
Arguments:
- material: int32 [6, 1536, 2048], P(None, 'grp', 'tile'), may hold values from 0 to 7
- conduct_table: float32 [8], replicated, may hold values from 1 to 20
- heat_sink: float32 [1536, 2048], P('grp', 'tile'), may hold values from 1 to 10
- heat_source: float32 [6, 1536, 2048], P(None, 'grp', 'tile'), may hold values from -120 to 120
- die_power: float32 [192, 128, 128], P(('grp', 'tile')), may hold values from -60 to 60
- die_conduct: float32 [192], P(('grp', 'tile')), may hold values from 1 to 8
- bond_conductance: float32 [192], P(('grp', 'tile')), may hold values from 0.5 to 4
- tile_place: int32 [192], P(('grp', 'tile')), may hold values from -1 to 191, as said below
Outputs:
- interposer_temp: float32 [6, 1536, 2048], P(None, 'grp', 'tile')
- die_temp: float32 [192, 128, 128], P(('grp', 'tile'))
Inputs may be any that keep to these rules, and one draw needn't show every extreme that they name: `tile_place`: -1 marks an empty slot; the other entries are distinct tile positions; one device holds all 6 of its slots filled and every device at least one.
All inputs are finite; a program needn't handle non-finite values.
Results may differ from a plain program's by a relative error of at most 0.0003.
Values sent between devices are 32-bit elements; how exact they have to be, the bound alone decides.
A program may use at most 192 MiB of HBM per device.

v0:
```python
import functools
import jax
import jax.numpy as jnp
from jax import lax
from jax.experimental import pallas as pl
from jax.experimental.pallas import tpu as pltpu
from jax.sharding import PartitionSpec as P

RATIO = 8
NU = 2
NC = 4
RELAX = 0.8
HALO = 4
TOP = 16
LANES = 128
MESH = pl.DeviceIdType.MESH
HIGHEST = lax.Precision.HIGHEST
DIRECTIONS = ((-1, 0), (1, 0), (0, -1), (0, 1), (-1, -1), (-1, 1), (1, -1), (1, 1))


def inverse(x):
    r = pl.reciprocal(x, approx=True)
    return r * (2.0 - x * r)


def harmonic(a, b):
    total = a + b
    return 2.0 * a * b * inverse(jnp.where(total > 0, total, 1.0))


def guarded_weight(d):
    return RELAX * inverse(jnp.where(d > 0, d, 1.0))


def iota(shape, dim):
    return lax.broadcasted_iota(jnp.int32, shape, dim)


def shift(x, amount, axis):
    return pltpu.roll(x, amount % x.shape[axis], axis)


def rows_at(ref, l, r, offset):
    if offset < 0:
        return ref.at[l, pl.ds(pl.multiple_of(r - 8, 8), 16), :][8 + offset : 16 + offset, :]
    return ref.at[l, pl.ds(r, 16), :][offset : 8 + offset, :]


def row_sums(fields):
    shape = fields[0].shape
    row = lax.broadcasted_iota(jnp.int32, shape, 0)
    xs = list(fields) + [jnp.zeros(shape, jnp.float32)] * (8 - len(fields))

    def merge(x, y, start, run):
        first = ((row - start + 8) % 8) % (2 * run) < run
        return jnp.where(first, x, y) + shift(jnp.where(first, y, x), -run, 0)

    z = [merge(xs[j], xs[j + 4], j, 4) for j in range(4)]
    y = [merge(z[j], z[j + 2], j, 2) for j in range(2)]
    return merge(y[0], y[1], 0, 1)


def dot(a, b):
    return jnp.dot(a, b, precision=HIGHEST, preferred_element_type=jnp.float32)


def kernel(
    grp_count,
    tile_count,
    material,
    table,
    heat_sink,
    source,
    die_power,
    die_conduct,
    bond,
    place,
    out,
    die_out,
    field,
    zx,
    zy,
    zz,
    diag,
    weight,
    ua,
    ub,
    packed,
    turned,
    from_side,
    from_corner,
    sums,
    folded,
    arrived,
    rough,
    rough_side,
    rough_row,
    rough_corner,
    dies,
    die_message,
    all_dies,
    die_fix,
    all_fixes,
    wide,
    solved,
    spread,
    send_sem,
    recv_sem,
    gather_send,
    gather_recv,
):
    layers, rows, cols = material.shape
    slots, edge, _ = die_power.shape
    cell = edge // RATIO
    down, across = rows // edge, cols // edge
    crows, ccols = rows // RATIO, cols // RATIO
    width = cols + LANES
    height = rows + 2 * TOP
    n_fields = 2 * layers + 1
    area = float(RATIO * RATIO)
    per = LANES // ccols
    count = grp_count * tile_count
    g = lax.axis_index("grp")
    t = lax.axis_index("tile")
    me = g * tile_count + t

    def peer(offset):
        other = lax.rem(me + offset, count)
        return other, (other // tile_count, lax.rem(other, tile_count))

    def exists(dy, dx):
        ok = jnp.bool_(True)
        if dy:
            ok = jnp.logical_and(ok, g > 0 if dy < 0 else g < grp_count - 1)
        if dx:
            ok = jnp.logical_and(ok, t > 0 if dx < 0 else t < tile_count - 1)
        return ok

    field[:, 0:TOP, :] = jnp.zeros((n_fields, TOP, width), jnp.float32)
    field[:, height - TOP : height, :] = jnp.zeros((n_fields, TOP, width), jnp.float32)
    from_side[...] = jnp.zeros_like(from_side)
    from_corner[...] = jnp.zeros_like(from_corner)
    rough_side[...] = jnp.zeros_like(rough_side)
    rough_row[...] = jnp.zeros_like(rough_row)
    rough_corner[...] = jnp.zeros_like(rough_corner)
    zx[:, 0:8, :] = jnp.zeros((layers, 8, width), jnp.float32)

    barrier = pltpu.get_barrier_semaphore()

    @pl.loop(1, count)
    def _(offset):
        pl.semaphore_signal(barrier, inc=1, device_id=peer(offset)[1], device_id_type=MESH)

    lane8 = iota((8, LANES), 1)

    @pl.loop(0, rows // 8)
    def _(i):
        r = pl.multiple_of(i * 8, 8)
        edges = jnp.zeros((8, LANES), jnp.float32)
        summed = []
        for f in range(n_fields):
            if f < layers:
                kind = material[f, pl.ds(r, 8), :]
                values = [jnp.full((8, cols), table[m], jnp.float32) for m in range(table.shape[0])]
                bit = 1
                while len(values) > 1:
                    odd = (kind & bit) != 0
                    values = [
                        jnp.where(odd, values[m + 1], values[m]) if m + 1 < len(values) else values[m]
                        for m in range(0, len(values), 2)
                    ]
                    bit *= 2
                x = values[0]
            elif f < 2 * layers:
                x = source[f - layers, pl.ds(r, 8), :]
            else:
                x = heat_sink[pl.ds(r, 8), :]
            field[f, pl.ds(TOP + r, 8), 0:cols] = x
            if f < layers or f == 2 * layers:
                summed.append(x)
            right = shift(x[:, cols - LANES :], HALO + HALO * f, 1)
            left = shift(x[:, :LANES], 64 + HALO * f, 1)
            in_right = (lane8 >= HALO * f) & (lane8 < HALO * (f + 1))
            in_left = (lane8 >= 64 + HALO * f) & (lane8 < 64 + HALO * (f + 1))
            edges = jnp.where(in_right, right, jnp.where(in_left, left, edges))
        packed[pl.ds(r, 8), :] = edges
        sums[pl.ds(r, 8), :] = row_sums(summed)

    turned[...] = packed[...].T

    pl.semaphore_wait(barrier, count - 1)

    depth = from_side.shape[1]

    def halo_copy(k):
        dy, dx = DIRECTIONS[k]
        if dx == 0:
            src = field.at[:, pl.ds(TOP if dy < 0 else height - TOP - 8, 8), pl.ds(0, cols)]
            dst = field.at[:, pl.ds(height - TOP if dy < 0 else TOP - 8, 8), pl.ds(0, cols)]
        elif dy == 0:
            src = turned.at[pl.ds(0 if dx > 0 else 64, depth), :]
            dst = from_side.at[0 if dx > 0 else 1]
        else:
            src = packed.at[pl.ds(0 if dy < 0 else rows - 8, 8), :]
            dst = from_corner.at[k - 4]
        return pltpu.make_async_remote_copy(
            src_ref=src, dst_ref=dst, send_sem=send_sem.at[k], recv_sem=recv_sem.at[k],
            device_id=(g + dy, t + dx), device_id_type=MESH,
        )

    def rough_copy(k, phase):
        dy, dx = DIRECTIONS[k]
        half = pl.ds(2 * phase, 2)
        if dy == 0:
            src = rough.at[half]
            dst = rough_side.at[k - 2, half]
        else:
            src = rough.at[half, pl.ds(0 if dy < 0 else crows - 8, 8), :]
            dst = (rough_row.at[k, half] if dx == 0 else rough_corner.at[k - 4, half])
        s = 8 * (phase + 1) + k
        return pltpu.make_async_remote_copy(
            src_ref=src, dst_ref=dst, send_sem=send_sem.at[s], recv_sem=recv_sem.at[s],
            device_id=(g + dy, t + dx), device_id_type=MESH,
        )

    def start_all(make):
        for k, (dy, dx) in enumerate(DIRECTIONS):
            pl.when(exists(dy, dx))(lambda k=k: make(k).start())

    def wait_all_recv(make):
        for k, (dy, dx) in enumerate(DIRECTIONS):
            pl.when(exists(-dy, -dx))(lambda k=k: make(k).wait_recv())

    def wait_all_send(make):
        for k, (dy, dx) in enumerate(DIRECTIONS):
            pl.when(exists(dy, dx))(lambda k=k: make(k).wait_send())

    start_all(halo_copy)

    srow, scol = iota((edge, edge), 0), iota((edge, edge), 1)
    one, none = jnp.float32(1.0), jnp.float32(0.0)
    sides = (
        jnp.where(srow > 0, one, none) + jnp.where(srow < edge - 1, one, none)
        + jnp.where(scol > 0, one, none) + jnp.where(scol < edge - 1, one, none)
    )

    def around(v):
        return (
            jnp.where(srow > 0, shift(v, 1, 0), 0.0)
            + jnp.where(srow < edge - 1, shift(v, -1, 0), 0.0)
            + jnp.where(scol > 0, shift(v, 1, 1), 0.0)
            + jnp.where(scol < edge - 1, shift(v, -1, 1), 0.0)
        )

    rows_in = (iota((cell, edge), 0) == iota((cell, edge), 1) // RATIO).astype(jnp.float32)
    message = jnp.zeros((cell, LANES), jnp.float32)
    row_m = iota((8, LANES), 0)
    params = jnp.full((8, LANES), -1.0, jnp.float32)
    for s in range(slots):
        c, b = die_conduct[s], bond[s]
        live = jnp.where(place[s] >= 0, 1.0, 0.0)
        p = die_power[s]
        d = c * sides + b
        wt = guarded_weight(d)
        v = wt * p
        v = (1.0 - RELAX) * v + wt * (p + c * around(v))
        dies[s] = v
        resid = live * (p + c * around(v) - d * v)
        cols_in = (
            iota((edge, LANES), 0) // RATIO + cell * s == iota((edge, LANES), 1)
        ).astype(jnp.float32)
        message = message + dot(dot(rows_in, resid), cols_in)
        mine = lane8 // cell == s
        value = jnp.where(
            row_m == 0, c, jnp.where(row_m == 1, b * area, place[s].astype(jnp.float32))
        )
        params = jnp.where(mine, value, params)
    die_message[0:cell, :] = message
    die_message[cell : cell + 8, :] = params
    all_dies[me] = die_message[...]

    def gather_copy(phase, other, slot, where):
        src, dst = (die_message, all_dies) if phase == 0 else (die_fix, all_fixes)
        return pltpu.make_async_remote_copy(
            src_ref=src, dst_ref=dst.at[slot],
            send_sem=gather_send.at[phase, other], recv_sem=gather_recv.at[phase, slot],
            device_id=where, device_id_type=MESH,
        )

    def gather_start(phase):
        @pl.loop(1, count)
        def _(offset):
            other, where = peer(offset)
            gather_copy(phase, other, me, where).start()

    def gather_wait(phase):
        @pl.loop(1, count)
        def _(offset):
            other, where = peer(offset)
            gather_copy(phase, other, other, where).wait()

    gather_start(0)

    def gathered(total, first_tile):
        pick = (iota((cols, LANES), 0) // RATIO == iota((cols, LANES), 1)).astype(jnp.float32)
        folded[...] = dot(sums[...], pick)
        for tile in range(2):
            result = jnp.zeros((crows, LANES), jnp.float32)
            for q in range(per):
                f = tile * per + q
                if f < total:
                    result = result + shift(folded[pl.ds(f, crows, stride=8), :], q * ccols, 1)
            rough[first_tile + tile] = result

    gathered(layers + 1, 0)
    start_all(lambda k: rough_copy(k, 0))

    wait_all_recv(halo_copy)
    pairs = []
    for f in range(n_fields):
        pairs.append(from_side[0, HALO * f : HALO * (f + 1), :])
        pairs.append(from_side[1, HALO * f : HALO * (f + 1), :])
    pairs.append(jnp.zeros((LANES - 2 * HALO * n_fields, rows), jnp.float32))
    arrived[TOP : height - TOP, :] = jnp.concatenate(pairs, axis=0).T

    def corner(x, y):
        tile = jnp.zeros((8, LANES), jnp.float32)
        for f in range(n_fields):
            at = lane8 - 2 * HALO * f
            tile = jnp.where((at >= 0) & (at < HALO), shift(x, HALO * f, 1), tile)
            tile = jnp.where(
                (at >= HALO) & (at < 2 * HALO), shift(y, HALO * f + HALO - 64, 1), tile
            )
        return tile

    arrived[0 : TOP - 8, :] = jnp.zeros((TOP - 8, LANES), jnp.float32)
    arrived[TOP - 8 : TOP, :] = corner(from_corner[3], from_corner[2])
    arrived[height - TOP : height - TOP + 8, :] = corner(from_corner[1], from_corner[0])
    arrived[height - TOP + 8 : height, :] = jnp.zeros((TOP - 8, LANES), jnp.float32)
    in_halo = (lane8 < HALO) | (lane8 >= LANES - HALO)

    def unpack(r):
        x = arrived[pl.ds(r, 8), :]
        for f in range(n_fields):
            field[f, pl.ds(r, 8), cols:width] = jnp.where(
                in_halo, shift(x, -HALO * (2 * f + 1), 1), 0.0
            )

    unpack(8)

    @pl.loop(1, height // 8 - 1)
    def _(i):
        r = pl.multiple_of(i * 8, 8)
        unpack(pl.multiple_of(r + 8, 8))
        ks = [field[l, pl.ds(r, 8), :] for l in range(layers)]
        below = None
        for l in range(layers):
            k = ks[l]
            fx = harmonic(k, rows_at(field, l, r, 1))
            fy = harmonic(k, shift(k, -1, 1))
            zx[l, pl.ds(r, 8), :] = fx
            zy[l, pl.ds(r, 8), :] = fy
            d = fx + rows_at(zx, l, r, -1) + fy + shift(fy, 1, 1)
            if l == 0:
                d = d + field[2 * layers, pl.ds(r, 8), :]
            else:
                d = d + below
            if l < layers - 1:
                below = harmonic(k, ks[l + 1])
                zz[l, pl.ds(r, 8), :] = below
                d = d + below
            diag[l, pl.ds(r, 8), :] = d
            wt = guarded_weight(d)
            weight[l, pl.ds(r, 8), :] = wt
            ua[l, pl.ds(r, 8), :] = wt * field[layers + l, pl.ds(r, 8), :]

    def pulled(u, r, l, us):
        centre = us[l]
        fx = zx[l, pl.ds(r, 8), :]
        fy = zy[l, pl.ds(r, 8), :]
        total = field[layers + l, pl.ds(r, 8), :]
        total = total + fx * rows_at(u, l, r, 1)
        total = total + rows_at(zx, l, r, -1) * rows_at(u, l, r, -1)
        total = total + fy * shift(centre, -1, 1) + shift(fy * centre, 1, 1)
        if l > 0:
            total = total + zz[l - 1, pl.ds(r, 8), :] * us[l - 1]
        if l < layers - 1:
            total = total + zz[l, pl.ds(r, 8), :] * us[l + 1]
        return total

    def sweep(u, store, first, last):
        @pl.loop(first, last)
        def _(i):
            r = pl.multiple_of(i * 8, 8)
            us = [u[l, pl.ds(r, 8), :] for l in range(layers)]
            for l in range(layers):
                total = pulled(u, r, l, us)
                new = (1.0 - RELAX) * us[l] + weight[l, pl.ds(r, 8), :] * total
                store(l, r, new)

    def into(ref):
        def store(l, r, new):
            ref[l, pl.ds(r, 8), :] = new

        return store

    sweep(ua, into(ub), 1, height // 8 - 1)

    @pl.loop(0, crows)
    def _(i):
        r = pl.multiple_of(i * 8 + TOP, 8)
        us = [ub[l, pl.ds(r, 8), :] for l in range(layers)]
        resids = []
        for l in range(layers):
            resid = pulled(ub, r, l, us) - diag[l, pl.ds(r, 8), :] * us[l]
            resids.append(resid[:, :cols])
        sums[pl.ds(pl.multiple_of(i * 8, 8), 8), :] = row_sums(resids)

    gathered(layers, 2)
    start_all(lambda k: rough_copy(k, 1))

    gather_wait(0)
    span = tile_count * across
    chigh = crows + 16
    parts = cell + 8
    spots = [(a, b) for a in range(-1, down + 1) for b in range(-1, across + 1)]
    wanted = []
    for a, b in spots:
        pr, pc = g * down + a, t * across + b
        inside = (pr >= 0) & (pr < grp_count * down) & (pc >= 0) & (pc < span)
        wanted.append(jnp.where(inside, pr * span + pc, -2).astype(jnp.float32))

    for lo in range(0, len(spots), across + 2):

        def add(d, acc, lo=lo):
            block = all_dies[d]
            where = block[cell + 2 : cell + 3, :]
            return tuple(
                a + jnp.where(where == wanted[lo + j], block, 0.0) for j, a in enumerate(acc)
            )

        acc = lax.fori_loop(
            0, count, add, tuple(jnp.zeros((parts, LANES), jnp.float32) for _ in range(across + 2))
        )
        lane_p = iota((parts, LANES), 1)
        line = jnp.zeros((parts, LANES), jnp.float32)
        for j in range(across + 2):
            x = acc[j]
            step = LANES // 2
            while step >= cell:
                x = x + shift(x, step, 1)
                step //= 2
            line = jnp.where(lane_p // cell == j, x, line)
        line = shift(line, 8 - cell, 1)
        a = lo // (across + 2) - 1
        if a == -1:
            first, size, off = 0, 8, cell - 8
        elif a == down:
            first, size, off = 8 + crows, 8, 0
        else:
            first, size, off = 8 + a * cell, cell, 0
        n = 2 * layers + 1
        wide[n, first : first + size, :] = line[off : off + size]
        wide[n + 1, first : first + size, :] = jnp.broadcast_to(
            line[cell : cell + 1], (size, LANES)
        )
        wide[n + 2, first : first + size, :] = jnp.broadcast_to(
            line[cell + 1 : cell + 2], (size, LANES)
        )

    for phase in range(2):
        wait_all_recv(lambda k: rough_copy(k, phase))
        for f in range(layers + 1 if phase == 0 else layers):
            tile, q = 2 * phase + f // per, f % per
            target = f if phase == 0 else layers + 1 + f

            def joined(left, middle, right, size):
                lane = iota((size, LANES), 1)
                x = shift(middle, 8 - ccols * q, 1)
                x = jnp.where((lane >= 8) & (lane < 8 + ccols), x, 0.0)
                x = jnp.where(lane < 8, shift(left, 8 - ccols - ccols * q, 1), x)
                return jnp.where(
                    (lane >= 8 + ccols) & (lane < 16 + ccols),
                    shift(right, 8 + ccols - ccols * q, 1),
                    x,
                )

            wide[target, 8 : 8 + crows, :] = joined(
                rough_side[1, tile], rough[tile], rough_side[0, tile], crows
            )
            wide[target, 0:8, :] = joined(
                rough_corner[3, tile], rough_row[1, tile], rough_corner[2, tile], 8
            )
            wide[target, 8 + crows : chigh, :] = joined(
                rough_corner[1, tile], rough_row[0, tile], rough_corner[0, tile], 8
            )

    kc = [wide[l] * (1.0 / area) for l in range(layers)]
    cx = [harmonic(k, shift(k, -1, 0)) for k in kc]
    cy = [harmonic(k, shift(k, -1, 1)) for k in kc]
    cz = [harmonic(kc[l], kc[l + 1]) * area for l in range(layers - 1)]
    top_rhs, top_c, top_b = (wide[2 * layers + 1 + j] for j in range(3))
    weights = []
    for l in range(layers):
        d = cx[l] + shift(cx[l], 1, 0) + cy[l] + shift(cy[l], 1, 1)
        if l == 0:
            d = d + wide[layers]
        else:
            d = d + cz[l - 1]
        d = d + (cz[l] if l < layers - 1 else top_b)
        weights.append(guarded_weight(d))
    crow = (iota((chigh, LANES), 0) + (cell - 8)) % cell
    ccol = (iota((chigh, LANES), 1) + (cell - 8)) % cell
    low_x, high_x = crow != 0, crow != cell - 1
    low_y, high_y = ccol != 0, ccol != cell - 1
    near = sum(jnp.where(m, one, none) for m in (low_x, high_x, low_y, high_y))
    top_d = top_c * near + top_b
    top_w = guarded_weight(top_d)
    errors = [weights[l] * wide[layers + 1 + l] for l in range(layers)]
    top = top_w * top_rhs
    for _ in range(NC - 1):
        new = []
        for l in range(layers):
            e = errors[l]
            total = wide[layers + 1 + l]
            total = total + cx[l] * shift(e, -1, 0) + shift(cx[l] * e, 1, 0)
            total = total + cy[l] * shift(e, -1, 1) + shift(cy[l] * e, 1, 1)
            if l > 0:
                total = total + cz[l - 1] * errors[l - 1]
            total = total + (cz[l] * errors[l + 1] if l < layers - 1 else top_b * top)
            new.append((1.0 - RELAX) * e + weights[l] * total)
        nearby = (
            jnp.where(low_x, shift(top, 1, 0), 0.0)
            + jnp.where(high_x, shift(top, -1, 0), 0.0)
            + jnp.where(low_y, shift(top, 1, 1), 0.0)
            + jnp.where(high_y, shift(top, -1, 1), 0.0)
        )
        top = top + top_w * (
            top_rhs + top_b * errors[layers - 1] + top_c * nearby - top_d * top
        )
        errors = new
    for l in range(layers):
        solved[l] = errors[l]

    lane_c = iota((cell, LANES), 1)
    fix = jnp.zeros((cell, LANES), jnp.float32)
    for a in range(down):
        piece = shift(top[8 + a * cell : 8 + (a + 1) * cell], a * ccols - 8, 1)
        fix = jnp.where(lane_c // ccols == a, piece, fix)
    die_fix[...] = fix
    all_fixes[me] = die_fix[...]
    gather_start(1)

    column = iota((LANES, width), 1)
    source_lane = jnp.where(column < cols + LANES // 2, 8 + column // RATIO, 7)
    pick = (iota((LANES, width), 0) == source_lane).astype(jnp.float32)
    for l in range(layers):
        spread[l] = dot(solved[l], pick)

    @pl.loop(1, height // 8 - 1)
    def _(i):
        r = pl.multiple_of(i * 8, 8)
        for l in range(layers):
            ub[l, pl.ds(r, 8), :] = ub[l, pl.ds(r, 8), :] + spread[l, pl.ds(i + 6, 1), :]

    sweep(ub, into(ua), 1, height // 8 - 1)

    def finish(l, r, new):
        out[l, pl.ds(r - TOP, 8), :] = new[:, :cols]

    sweep(ua, finish, TOP // 8, (height - TOP) // 8)

    gather_wait(1)
    codes = []
    for s in range(slots):
        spot = jnp.maximum(place[s], 0)
        pr, pc = spot // span, lax.rem(spot, span)
        target = (pr // down) * tile_count + pc // across
        local = lax.rem(pr, down) * across + lax.rem(pc, across)
        codes.append(jnp.where(place[s] >= 0, target * 8 + local, -1))
    group = lane_c // cell

    def collect(d, acc):
        block = all_fixes[d]
        code = group + d * 8
        return tuple(a + jnp.where(code == codes[s], block, 0.0) for s, a in enumerate(acc))

    fixes = lax.fori_loop(
        0, count, collect, tuple(jnp.zeros((cell, LANES), jnp.float32) for _ in range(slots))
    )
    rows_out = (iota((edge, cell), 0) // RATIO == iota((edge, cell), 1)).astype(jnp.float32)
    cols_out = (iota((LANES, edge), 0) == iota((LANES, edge), 1) // RATIO).astype(jnp.float32)
    for s in range(slots):
        x = fixes[s]
        step = LANES // 2
        while step >= cell:
            x = x + shift(x, step, 1)
            step //= 2
        c, b = die_conduct[s], bond[s]
        live = jnp.where(place[s] >= 0, 1.0, 0.0)
        p = die_power[s]
        wt = guarded_weight(c * sides + b)
        v = dies[s] + live * dot(rows_out, dot(x, cols_out))
        for _ in range(NU):
            v = (1.0 - RELAX) * v + wt * (p + c * around(v))
        die_out[s] = live * v

    wait_all_send(halo_copy)
    for phase in range(2):
        wait_all_send(lambda k: rough_copy(k, phase))


def per_device(grp_count, tile_count, *args):
    material, die_power = args[0], args[4]
    layers, rows, cols = material.shape
    slots, edge, _ = die_power.shape
    cell = edge // RATIO
    crows = rows // RATIO
    width, height = cols + LANES, rows + 2 * TOP
    count = grp_count * tile_count
    n_fields = 2 * layers + 1
    depth = -(-n_fields * HALO // 8) * 8
    vmem = pl.BlockSpec(memory_space=pltpu.VMEM)
    smem = pl.BlockSpec(memory_space=pltpu.SMEM)
    f32 = jnp.float32

    def scratch(*shape):
        return pltpu.VMEM(shape, f32)

    grid = (layers, height, width)
    return pl.pallas_call(
        functools.partial(kernel, grp_count, tile_count),
        out_shape=(
            jax.ShapeDtypeStruct((layers, rows, cols), f32),
            jax.ShapeDtypeStruct((slots, edge, edge), f32),
        ),
        in_specs=[vmem, smem, vmem, vmem, vmem, smem, smem, smem],
        out_specs=(vmem, vmem),
        scratch_shapes=[
            scratch(n_fields, height, width),
            scratch(*grid),
            scratch(*grid),
            scratch(layers - 1, height, width),
            scratch(*grid),
            scratch(*grid),
            scratch(*grid),
            scratch(*grid),
            scratch(rows, LANES),
            scratch(LANES, rows),
            scratch(2, depth, rows),
            scratch(4, 8, LANES),
            scratch(rows, cols),
            scratch(rows, LANES),
            scratch(height, LANES),
            scratch(4, crows, LANES),
            scratch(2, 4, crows, LANES),
            scratch(2, 4, 8, LANES),
            scratch(4, 4, 8, LANES),
            scratch(slots, edge, edge),
            scratch(cell + 8, LANES),
            scratch(count, cell + 8, LANES),
            scratch(cell, LANES),
            scratch(count, cell, LANES),
            scratch(n_fields + 3, crows + 16, LANES),
            scratch(layers, crows + 16, LANES),
            scratch(layers, crows + 16, width),
            pltpu.SemaphoreType.DMA((24,)),
            pltpu.SemaphoreType.DMA((24,)),
            pltpu.SemaphoreType.DMA((2, count)),
            pltpu.SemaphoreType.DMA((2, count)),
        ],
        compiler_params=pltpu.CompilerParams(
            collective_id=0, has_side_effects=True, vmem_limit_bytes=60 * 1024 * 1024
        ),
    )(*args)


def solution(mesh):
    placed = (
        P(None, "grp", "tile"),
        P(),
        P("grp", "tile"),
        P(None, "grp", "tile"),
        P(("grp", "tile"), None, None),
        P(("grp", "tile")),
        P(("grp", "tile")),
        P(("grp", "tile")),
    )
    return jax.shard_map(
        functools.partial(per_device, mesh.shape["grp"], mesh.shape["tile"]),
        mesh=mesh,
        in_specs=placed,
        out_specs=(P(None, "grp", "tile"), P(("grp", "tile"), None, None)),
        check_vma=False,
    )
```

profile of v0, /device:TPU:0, one launch (start us, length us, event | category | flops | bytes accessed | tf_op | source)
XLA Modules:
  0.0 76.7 jit_solution(520599357282264739)
XLA Ops:
  0.6 71.9 %shard_map.95 = (f32[6,384,256]{2,1,0:T(8,128)}, f32[6,128,128]{2,1,0:T(8,128)}) custom-call(s32[6,384,256]{2,1,0:T(8,128)} %material.1, f32[8]{0:T(128)} %table.1, f32[384,256]{1,0:T(8,128)} %heat_sink.1, f32[6,384,256]{2,1,0:T(8,128)} %source.1, f32[6,128,128]{2,1,0:T(8,128)} %die_power.1, f32[6]{0:T(128)} %die_conduct.1, f32[6]{0:T(128)} %bond.1, s32[6]{0:T(128)} %place.1), custom_call_target="tpu_custom_call" | custom-call | tf_op jit(solution)/shard_map/pallas_call | solution.py:631
  72.5 0.0 copy-start
  72.5 3.4 %copy.12 = f32[6,384,256]{2,1,0:T(8,128)} copy(f32[6,384,256]{2,1,0:T(8,128)} %get-tuple-element.4) | data formatting | bytes 4718592
  75.9 0.0 copy-done
  75.9 0.7 copy.13
Async XLA Ops:
  72.5 3.4 %copy-start = (f32[6,128,128]{2,1,0:T(8,128)S(1)}, f32[6,128,128]{2,1,0:T(8,128)}, u32[]{:S(2)}) copy-start(f32[6,128,128]{2,1,0:T(8,128)} %get-tuple-element.5) | copy-start | bytes 1179652
where the time goes:
time: 77.2 us; the launch traced here: 76.7 us
  Pallas kernels  71.9 us (93%)
  local copies, waits for them, and re-layouts  4.16 us (5%)
    pallas_call x1, Pallas kernels, per_device(): pl.pallas_call(functools.partial(kernel, grp_count, tile_count), out_shap...  71.9 us
    unnamed x4, local copies, waits for them, and re-layouts  4.16 us

commit v1 on v0

--- a/solution.py
+++ b/solution.py
@@ -13,14 +13,17 @@
 HALO = 4
 TOP = 16
 LANES = 128
+FAR = 1e30
+TINY = 1e-25
+UNROLL = 2
 MESH = pl.DeviceIdType.MESH
 HIGHEST = lax.Precision.HIGHEST
-DIRECTIONS = ((-1, 0), (1, 0), (0, -1), (0, 1), (-1, -1), (-1, 1), (1, -1), (1, 1))
+DIRECTIONS = ((-1, 0), (1, 0), (0, -1), (0, 1), (-1, -1), (-1, 1), (1, -1), (1, 1), (-1, 0), (1, 0))
+N_ROUGH = 8
 
 
 def inverse(x):
-    r = pl.reciprocal(x, approx=True)
-    return r * (2.0 - x * r)
+    return pltpu.reciprocal(x, approx=True)
 
 
 def harmonic(a, b):
@@ -29,7 +32,7 @@
 
 
 def guarded_weight(d):
-    return RELAX * inverse(jnp.where(d > 0, d, 1.0))
+    return RELAX * inverse(jnp.where(d > TINY, d, 1.0))
 
 
 def iota(shape, dim):
@@ -38,12 +41,6 @@
 
 def shift(x, amount, axis):
     return pltpu.roll(x, amount % x.shape[axis], axis)
-
-
-def rows_at(ref, l, r, offset):
-    if offset < 0:
-        return ref.at[l, pl.ds(pl.multiple_of(r - 8, 8), 16), :][8 + offset : 16 + offset, :]
-    return ref.at[l, pl.ds(r, 16), :][offset : 8 + offset, :]
 
 
 def row_sums(fields):
@@ -58,6 +55,15 @@
     z = [merge(xs[j], xs[j + 4], j, 4) for j in range(4)]
     y = [merge(z[j], z[j + 2], j, 2) for j in range(2)]
     return merge(y[0], y[1], 0, 1)
+
+
+def two_part_dot(a, b):
+    high = a.astype(jnp.bfloat16)
+    low = (a - high.astype(jnp.float32)).astype(jnp.bfloat16)
+    b = b.astype(jnp.bfloat16)
+    return jnp.dot(high, b, preferred_element_type=jnp.float32) + jnp.dot(
+        low, b, preferred_element_type=jnp.float32
+    )
 
 
 def dot(a, b):
@@ -88,10 +94,16 @@
     packed,
     turned,
     from_side,
-    from_corner,
+    outer,
+    strip,
+    sx,
+    sy,
+    sz,
+    sw,
+    su,
+    lines,
     sums,
     folded,
-    arrived,
     rough,
     rough_side,
     rough_row,
@@ -102,7 +114,6 @@
     die_fix,
     all_fixes,
     wide,
-    solved,
     spread,
     send_sem,
     recv_sem,
@@ -114,7 +125,8 @@
     cell = edge // RATIO
     down, across = rows // edge, cols // edge
     crows, ccols = rows // RATIO, cols // RATIO
-    width = cols + LANES
+    panes = cols // LANES
+    long = rows + LANES
     height = rows + 2 * TOP
     n_fields = 2 * layers + 1
     area = float(RATIO * RATIO)
@@ -136,14 +148,19 @@
             ok = jnp.logical_and(ok, t > 0 if dx < 0 else t < tile_count - 1)
         return ok
 
-    field[:, 0:TOP, :] = jnp.zeros((n_fields, TOP, width), jnp.float32)
-    field[:, height - TOP : height, :] = jnp.zeros((n_fields, TOP, width), jnp.float32)
-    from_side[...] = jnp.zeros_like(from_side)
-    from_corner[...] = jnp.zeros_like(from_corner)
+    for top in (0, height - TOP):
+        field[0:layers, :, top : top + TOP, :] = jnp.full((layers, panes, TOP, LANES), FAR, jnp.float32)
+        field[layers:n_fields, :, top : top + TOP, :] = jnp.zeros(
+            (n_fields - layers, panes, TOP, LANES), jnp.float32
+        )
+    cut = HALO * layers
+    from_side[:, 0:cut, :] = jnp.full((2, cut, rows), FAR, jnp.float32)
+    from_side[:, cut:, :] = jnp.zeros((2, from_side.shape[1] - cut, rows), jnp.float32)
+    outer[...] = jnp.where(iota(outer.shape, 2) % 64 < cut, FAR, 0.0)
     rough_side[...] = jnp.zeros_like(rough_side)
     rough_row[...] = jnp.zeros_like(rough_row)
     rough_corner[...] = jnp.zeros_like(rough_corner)
-    zx[:, 0:8, :] = jnp.zeros((layers, 8, width), jnp.float32)
+    zx[:, :, 0:8, :] = jnp.zeros((layers, panes, 8, LANES), jnp.float32)
 
     barrier = pltpu.get_barrier_semaphore()
 
@@ -152,39 +169,53 @@
         pl.semaphore_signal(barrier, inc=1, device_id=peer(offset)[1], device_id_type=MESH)
 
     lane8 = iota((8, LANES), 1)
+    sub8 = iota((8, LANES), 0)
+
+    def right_lane(f):
+        return HALO * f
+
+    def left_lane(f):
+        return 64 + 8 * (f // 2) + HALO * (1 - f % 2)
+
+    doubled = [jnp.full((8, LANES), 2.0 * table[m], jnp.float32) for m in range(table.shape[0])]
 
     @pl.loop(0, rows // 8)
     def _(i):
         r = pl.multiple_of(i * 8, 8)
         edges = jnp.zeros((8, LANES), jnp.float32)
-        summed = []
+        summed = [[] for _ in range(panes)]
         for f in range(n_fields):
-            if f < layers:
-                kind = material[f, pl.ds(r, 8), :]
-                values = [jnp.full((8, cols), table[m], jnp.float32) for m in range(table.shape[0])]
-                bit = 1
-                while len(values) > 1:
-                    odd = (kind & bit) != 0
-                    values = [
-                        jnp.where(odd, values[m + 1], values[m]) if m + 1 < len(values) else values[m]
-                        for m in range(0, len(values), 2)
-                    ]
-                    bit *= 2
-                x = values[0]
-            elif f < 2 * layers:
-                x = source[f - layers, pl.ds(r, 8), :]
-            else:
-                x = heat_sink[pl.ds(r, 8), :]
-            field[f, pl.ds(TOP + r, 8), 0:cols] = x
-            if f < layers or f == 2 * layers:
-                summed.append(x)
-            right = shift(x[:, cols - LANES :], HALO + HALO * f, 1)
-            left = shift(x[:, :LANES], 64 + HALO * f, 1)
-            in_right = (lane8 >= HALO * f) & (lane8 < HALO * (f + 1))
-            in_left = (lane8 >= 64 + HALO * f) & (lane8 < 64 + HALO * (f + 1))
-            edges = jnp.where(in_right, right, jnp.where(in_left, left, edges))
+            xs = []
+            for p in range(panes):
+                part = slice(p * LANES, (p + 1) * LANES)
+                if f < layers:
+                    kind = material[f, pl.ds(r, 8), part]
+                    values = list(doubled)
+                    bit = 1
+                    while len(values) > 1:
+                        odd = (kind & bit) != 0
+                        values = [
+                            jnp.where(odd, values[m + 1], values[m]) if m + 1 < len(values) else values[m]
+                            for m in range(0, len(values), 2)
+                        ]
+                        bit *= 2
+                    summed[p].append(values[0])
+                    x = inverse(values[0])
+                elif f < 2 * layers:
+                    x = source[f - layers, pl.ds(r, 8), part]
+                else:
+                    x = heat_sink[pl.ds(r, 8), part]
+                    summed[p].append(x)
+                field[f, p, pl.ds(TOP + r, 8), :] = x
+                xs.append(x)
+            a, b = right_lane(f), left_lane(f)
+            right = shift(xs[-1], HALO + a, 1)
+            left = shift(xs[0], b, 1)
+            edges = jnp.where((lane8 >= a) & (lane8 < a + HALO), right, edges)
+            edges = jnp.where((lane8 >= b) & (lane8 < b + HALO), left, edges)
         packed[pl.ds(r, 8), :] = edges
-        sums[pl.ds(r, 8), :] = row_sums(summed)
+        for p in range(panes):
+            sums[pl.ds(r, 8), p * LANES : (p + 1) * LANES] = row_sums(summed[p])
 
     turned[...] = packed[...].T
 
@@ -194,15 +225,16 @@
 
     def halo_copy(k):
         dy, dx = DIRECTIONS[k]
-        if dx == 0:
-            src = field.at[:, pl.ds(TOP if dy < 0 else height - TOP - 8, 8), pl.ds(0, cols)]
-            dst = field.at[:, pl.ds(height - TOP if dy < 0 else TOP - 8, 8), pl.ds(0, cols)]
+        if k < 2:
+            src = field.at[:, :, pl.ds(TOP if dy < 0 else height - TOP - 8, 8), :]
+            dst = field.at[:, :, pl.ds(height - TOP if dy < 0 else TOP - 8, 8), :]
         elif dy == 0:
             src = turned.at[pl.ds(0 if dx > 0 else 64, depth), :]
             dst = from_side.at[0 if dx > 0 else 1]
         else:
             src = packed.at[pl.ds(0 if dy < 0 else rows - 8, 8), :]
-            dst = from_corner.at[k - 4]
+            which = 2 if dx == 0 else (0 if dx > 0 else 1)
+            dst = outer.at[which, pl.ds(0 if dy < 0 else LANES - 8, 8), :]
         return pltpu.make_async_remote_copy(
             src_ref=src, dst_ref=dst, send_sem=send_sem.at[k], recv_sem=recv_sem.at[k],
             device_id=(g + dy, t + dx), device_id_type=MESH,
@@ -217,25 +249,25 @@
         else:
             src = rough.at[half, pl.ds(0 if dy < 0 else crows - 8, 8), :]
             dst = (rough_row.at[k, half] if dx == 0 else rough_corner.at[k - 4, half])
-        s = 8 * (phase + 1) + k
+        s = len(DIRECTIONS) + N_ROUGH * phase + k
         return pltpu.make_async_remote_copy(
             src_ref=src, dst_ref=dst, send_sem=send_sem.at[s], recv_sem=recv_sem.at[s],
             device_id=(g + dy, t + dx), device_id_type=MESH,
         )
 
-    def start_all(make):
-        for k, (dy, dx) in enumerate(DIRECTIONS):
+    def start_all(make, n):
+        for k, (dy, dx) in enumerate(DIRECTIONS[:n]):
             pl.when(exists(dy, dx))(lambda k=k: make(k).start())
 
-    def wait_all_recv(make):
-        for k, (dy, dx) in enumerate(DIRECTIONS):
+    def wait_all_recv(make, n):
+        for k, (dy, dx) in enumerate(DIRECTIONS[:n]):
             pl.when(exists(-dy, -dx))(lambda k=k: make(k).wait_recv())
 
-    def wait_all_send(make):
-        for k, (dy, dx) in enumerate(DIRECTIONS):
+    def wait_all_send(make, n):
+        for k, (dy, dx) in enumerate(DIRECTIONS[:n]):
             pl.when(exists(dy, dx))(lambda k=k: make(k).wait_send())
 
-    start_all(halo_copy)
+    start_all(halo_copy, len(DIRECTIONS))
 
     srow, scol = iota((edge, edge), 0), iota((edge, edge), 1)
     one, none = jnp.float32(1.0), jnp.float32(0.0)
@@ -303,7 +335,7 @@
 
     def gathered(total, first_tile):
         pick = (iota((cols, LANES), 0) // RATIO == iota((cols, LANES), 1)).astype(jnp.float32)
-        folded[...] = dot(sums[...], pick)
+        folded[...] = two_part_dot(sums[...], pick)
         for tile in range(2):
             result = jnp.zeros((crows, LANES), jnp.float32)
             for q in range(per):
@@ -313,111 +345,201 @@
             rough[first_tile + tile] = result
 
     gathered(layers + 1, 0)
-    start_all(lambda k: rough_copy(k, 0))
-
-    wait_all_recv(halo_copy)
-    pairs = []
+    start_all(lambda k: rough_copy(k, 0), N_ROUGH)
+
+    wait_all_recv(halo_copy, len(DIRECTIONS))
+    extra = [outer[j].T for j in range(3)]
+
+    def woven(near, far, f, first):
+        size = near.shape[1]
+        lower = iota((8, size), 0) < HALO
+        m = f // 2 * 8
+        a = (far if first else near)[m : m + 8]
+        b = (near if first else far)[m : m + 8]
+        return (
+            jnp.where(lower, a, b) if f % 2 == 0 else shift(jnp.where(lower, b, a), HALO, 0)
+        )
+
     for f in range(n_fields):
-        pairs.append(from_side[0, HALO * f : HALO * (f + 1), :])
-        pairs.append(from_side[1, HALO * f : HALO * (f + 1), :])
-    pairs.append(jnp.zeros((LANES - 2 * HALO * n_fields, rows), jnp.float32))
-    arrived[TOP : height - TOP, :] = jnp.concatenate(pairs, axis=0).T
-
-    def corner(x, y):
-        tile = jnp.zeros((8, LANES), jnp.float32)
-        for f in range(n_fields):
-            at = lane8 - 2 * HALO * f
-            tile = jnp.where((at >= 0) & (at < HALO), shift(x, HALO * f, 1), tile)
-            tile = jnp.where(
-                (at >= HALO) & (at < 2 * HALO), shift(y, HALO * f + HALO - 64, 1), tile
+        for side in range(2):
+            at = 64 if side == 0 else 0
+            strip[side, f, :, 0:rows] = woven(
+                turned[at : at + depth, :], from_side[side], f, side == 0
             )
-        return tile
-
-    arrived[0 : TOP - 8, :] = jnp.zeros((TOP - 8, LANES), jnp.float32)
-    arrived[TOP - 8 : TOP, :] = corner(from_corner[3], from_corner[2])
-    arrived[height - TOP : height - TOP + 8, :] = corner(from_corner[1], from_corner[0])
-    arrived[height - TOP + 8 : height, :] = jnp.zeros((TOP - 8, LANES), jnp.float32)
-    in_halo = (lane8 < HALO) | (lane8 >= LANES - HALO)
-
-    def unpack(r):
-        x = arrived[pl.ds(r, 8), :]
-        for f in range(n_fields):
-            field[f, pl.ds(r, 8), cols:width] = jnp.where(
-                in_halo, shift(x, -HALO * (2 * f + 1), 1), 0.0
+            strip[side, f, :, rows:long] = woven(
+                extra[2][at : at + depth], extra[side][64 - at : 64 - at + depth], f, side == 0
             )
 
-    unpack(8)
-
-    @pl.loop(1, height // 8 - 1)
+    def strip_total(side, l, us):
+        u, fx, fy = us[l], sx[side, l], sy[side, l]
+        total = strip[side, layers + l] + fx * shift(u, -1, 1) + shift(fx * u, 1, 1)
+        total = total + fy * shift(u, -1, 0) + shift(fy * u, 1, 0)
+        if l > 0:
+            total = total + sz[side, l - 1] * us[l - 1]
+        if l < layers - 1:
+            total = total + sz[side, l] * us[l + 1]
+        return total
+
+    def strip_sweep(side, us):
+        return [
+            (1.0 - RELAX) * us[l] + sw[side, l] * strip_total(side, l, us) for l in range(layers)
+        ]
+
+    def lay_lines(k, rows_of):
+        x = jnp.concatenate(
+            rows_of + [jnp.zeros((LANES - 8 * layers, long), jnp.float32)], axis=0
+        ).T
+        lines[k, TOP : TOP + rows + 8, :] = x[0 : rows + 8]
+        lines[k, TOP - 8 : TOP, :] = x[long - 8 : long]
+
+    sub_long = iota((8, long), 0)
+
+    def line_rows(l, fields, has_face):
+        parts = []
+        if has_face:
+            parts = [shift(sy[1, l], -3, 0), shift(sy[0, l], -2, 0)]
+        for left, right in fields:
+            q = len(parts)
+            parts.append(shift(right[l], q - 4, 0))
+            parts.append(shift(sy[0, l] * left[l], q - 2, 0))
+        x = parts[0]
+        for q in range(1, len(parts)):
+            x = jnp.where(sub_long == q, parts[q], x)
+        return x
+
+    smooth = []
+    for side in range(2):
+        below = None
+        us = []
+        for l in range(layers):
+            k = strip[side, l]
+            fx = inverse(k + shift(k, -1, 1))
+            fy = inverse(k + shift(k, -1, 0))
+            sx[side, l] = fx
+            sy[side, l] = fy
+            d = fx + shift(fx, 1, 1) + fy + shift(fy, 1, 0)
+            d = d + (strip[side, 2 * layers] if l == 0 else below)
+            if l < layers - 1:
+                below = inverse(k + strip[side, l + 1])
+                sz[side, l] = below
+                d = d + below
+            wt = guarded_weight(d)
+            sw[side, l] = wt
+            us.append(wt * strip[side, layers + l])
+        new = strip_sweep(side, us)
+        for l in range(layers):
+            su[side, l] = new[l]
+        smooth.append((us, new))
+    fields = list(zip(*smooth))
+    lay_lines(0, [line_rows(l, fields, True) for l in range(layers)])
+
+    first8, last8 = lane8 == 0, lane8 == LANES - 1
+
+    def from_right(xs, p, end):
+        turn = shift(xs[p], -1, 1)
+        if p < panes - 1:
+            return jnp.where(last8, shift(xs[p + 1], -1, 1), turn)
+        return turn if end is None else jnp.where(last8, end, turn)
+
+    def from_left(xs, p, end):
+        return jnp.where(first8, end if p == 0 else shift(xs[p - 1], 1, 1), shift(xs[p], 1, 1))
+
+    def line_ends(line, l, q):
+        return shift(line, -(8 * l + 2 * q + 1), 1)
+
+    @pl.loop(1, height // 8 - 1, unroll=UNROLL)
     def _(i):
         r = pl.multiple_of(i * 8, 8)
-        unpack(pl.multiple_of(r + 8, 8))
-        ks = [field[l, pl.ds(r, 8), :] for l in range(layers)]
-        below = None
+        here = pl.ds(r, 8)
+        line = lines[0, here, :]
+        ks = [[field[l, p, here, :] for p in range(panes)] for l in range(layers)]
+        fxs = []
+        for l in range(layers):
+            fxs.append([])
+            for p in range(panes):
+                fx = inverse(ks[l][p] + field[l, p, pl.ds(r + 1, 8), :])
+                zx[l, p, here, :] = fx
+                fxs[l].append(fx)
+        below = [None] * panes
         for l in range(layers):
             k = ks[l]
-            fx = harmonic(k, rows_at(field, l, r, 1))
-            fy = harmonic(k, shift(k, -1, 1))
-            zx[l, pl.ds(r, 8), :] = fx
-            zy[l, pl.ds(r, 8), :] = fy
-            d = fx + rows_at(zx, l, r, -1) + fy + shift(fy, 1, 1)
-            if l == 0:
-                d = d + field[2 * layers, pl.ds(r, 8), :]
-            else:
-                d = d + below
+            ends = line_ends(line, l, 0)
+            fys = [inverse(k[p] + from_right(k, p, None)) for p in range(panes)]
+            fys[-1] = jnp.where(last8, ends, fys[-1])
+            for p in range(panes):
+                fy = fys[p]
+                zy[l, p, here, :] = fy
+                d = fxs[l][p] + zx[l, p, pl.ds(r - 1, 8), :] + fy + from_left(fys, p, ends)
+                d = d + (field[2 * layers, p, here, :] if l == 0 else below[p])
+                if l < layers - 1:
+                    below[p] = inverse(k[p] + ks[l + 1][p])
+                    zz[l, p, here, :] = below[p]
+                    d = d + below[p]
+                diag[l, p, here, :] = d
+                wt = guarded_weight(d)
+                weight[l, p, here, :] = wt
+                ua[l, p, here, :] = wt * field[layers + l, p, here, :]
+
+    def pulled(u, r, l, us, line, q):
+        here = pl.ds(r, 8)
+        fys = [zy[l, p, here, :] for p in range(panes)]
+        flows = [fys[p] * us[l][p] for p in range(panes)]
+        ends = line_ends(line, l, q)
+        totals = []
+        for p in range(panes):
+            total = field[layers + l, p, here, :]
+            total = total + zx[l, p, here, :] * u[l, p, pl.ds(r + 1, 8), :]
+            total = total + zx[l, p, pl.ds(r - 1, 8), :] * u[l, p, pl.ds(r - 1, 8), :]
+            total = total + fys[p] * from_right(us[l], p, ends) + from_left(flows, p, ends)
+            if l > 0:
+                total = total + zz[l - 1, p, here, :] * us[l - 1][p]
             if l < layers - 1:
-                below = harmonic(k, ks[l + 1])
-                zz[l, pl.ds(r, 8), :] = below
-                d = d + below
-            diag[l, pl.ds(r, 8), :] = d
-            wt = guarded_weight(d)
-            weight[l, pl.ds(r, 8), :] = wt
-            ua[l, pl.ds(r, 8), :] = wt * field[layers + l, pl.ds(r, 8), :]
-
-    def pulled(u, r, l, us):
-        centre = us[l]
-        fx = zx[l, pl.ds(r, 8), :]
-        fy = zy[l, pl.ds(r, 8), :]
-        total = field[layers + l, pl.ds(r, 8), :]
-        total = total + fx * rows_at(u, l, r, 1)
-        total = total + rows_at(zx, l, r, -1) * rows_at(u, l, r, -1)
-        total = total + fy * shift(centre, -1, 1) + shift(fy * centre, 1, 1)
-        if l > 0:
-            total = total + zz[l - 1, pl.ds(r, 8), :] * us[l - 1]
-        if l < layers - 1:
-            total = total + zz[l, pl.ds(r, 8), :] * us[l + 1]
-        return total
-
-    def sweep(u, store, first, last):
-        @pl.loop(first, last)
+                total = total + zz[l, p, here, :] * us[l + 1][p]
+            totals.append(total)
+        return totals
+
+    def layers_at(u, r):
+        return [[u[l, p, pl.ds(r, 8), :] for p in range(panes)] for l in range(layers)]
+
+    def sweep(u, store, first, last, k, q):
+        @pl.loop(first, last, unroll=UNROLL)
         def _(i):
             r = pl.multiple_of(i * 8, 8)
-            us = [u[l, pl.ds(r, 8), :] for l in range(layers)]
+            us = layers_at(u, r)
+            line = lines[k, pl.ds(r, 8), :]
             for l in range(layers):
-                total = pulled(u, r, l, us)
-                new = (1.0 - RELAX) * us[l] + weight[l, pl.ds(r, 8), :] * total
-                store(l, r, new)
+                totals = pulled(u, r, l, us, line, q)
+                for p in range(panes):
+                    store(
+                        l, p, r,
+                        (1.0 - RELAX) * us[l][p] + weight[l, p, pl.ds(r, 8), :] * totals[p],
+                    )
 
     def into(ref):
-        def store(l, r, new):
-            ref[l, pl.ds(r, 8), :] = new
+        def store(l, p, r, new):
+            ref[l, p, pl.ds(r, 8), :] = new
 
         return store
 
-    sweep(ua, into(ub), 1, height // 8 - 1)
-
-    @pl.loop(0, crows)
+    sweep(ua, into(ub), 1, height // 8 - 1, 0, 1)
+
+    @pl.loop(0, crows, unroll=UNROLL)
     def _(i):
         r = pl.multiple_of(i * 8 + TOP, 8)
-        us = [ub[l, pl.ds(r, 8), :] for l in range(layers)]
-        resids = []
+        us = layers_at(ub, r)
+        line = lines[0, pl.ds(r, 8), :]
+        resids = [[] for _ in range(panes)]
         for l in range(layers):
-            resid = pulled(ub, r, l, us) - diag[l, pl.ds(r, 8), :] * us[l]
-            resids.append(resid[:, :cols])
-        sums[pl.ds(pl.multiple_of(i * 8, 8), 8), :] = row_sums(resids)
+            totals = pulled(ub, r, l, us, line, 2)
+            for p in range(panes):
+                resids[p].append(totals[p] - diag[l, p, pl.ds(r, 8), :] * us[l][p])
+        for p in range(panes):
+            sums[pl.ds(pl.multiple_of(i * 8, 8), 8), p * LANES : (p + 1) * LANES] = row_sums(
+                resids[p]
+            )
 
     gathered(layers, 2)
-    start_all(lambda k: rough_copy(k, 1))
+    start_all(lambda k: rough_copy(k, 1), N_ROUGH)
 
     gather_wait(0)
     span = tile_count * across
@@ -469,7 +591,7 @@
         )
 
     for phase in range(2):
-        wait_all_recv(lambda k: rough_copy(k, phase))
+        wait_all_recv(lambda k: rough_copy(k, phase), N_ROUGH)
         for f in range(layers + 1 if phase == 0 else layers):
             tile, q = 2 * phase + f // per, f % per
             target = f if phase == 0 else layers + 1 + f
@@ -495,7 +617,7 @@
                 rough_corner[1, tile], rough_row[0, tile], rough_corner[0, tile], 8
             )
 
-    kc = [wide[l] * (1.0 / area) for l in range(layers)]
+    kc = [wide[l] * (0.5 / area) for l in range(layers)]
     cx = [harmonic(k, shift(k, -1, 0)) for k in kc]
     cy = [harmonic(k, shift(k, -1, 1)) for k in kc]
     cz = [harmonic(kc[l], kc[l + 1]) * area for l in range(layers - 1)]
@@ -539,9 +661,6 @@
             top_rhs + top_b * errors[layers - 1] + top_c * nearby - top_d * top
         )
         errors = new
-    for l in range(layers):
-        solved[l] = errors[l]
-
     lane_c = iota((cell, LANES), 1)
     fix = jnp.zeros((cell, LANES), jnp.float32)
     for a in range(down):
@@ -551,24 +670,47 @@
     all_fixes[me] = die_fix[...]
     gather_start(1)
 
-    column = iota((LANES, width), 1)
-    source_lane = jnp.where(column < cols + LANES // 2, 8 + column // RATIO, 7)
-    pick = (iota((LANES, width), 0) == source_lane).astype(jnp.float32)
+    pick = (iota((LANES, cols), 0) == 8 + iota((LANES, cols), 1) // RATIO).astype(jnp.float32)
+    fine = two_part_dot(jnp.concatenate(errors, axis=0), pick)
     for l in range(layers):
-        spread[l] = dot(solved[l], pick)
+        for p in range(panes):
+            spread[l, p] = fine[l * chigh : (l + 1) * chigh, p * LANES : (p + 1) * LANES]
+    lane_s = iota((LANES, LANES), 1)
+    wanted_lane = jnp.where(lane_s % 8 < HALO, 7, 8) + jnp.where(lane_s % 16 < 8, 0, ccols)
+    wanted_lane = jnp.where(
+        iota((LANES, LANES), 0) == wanted_lane, lane_s // 16, -1
+    )
+    sides_of = jnp.zeros((chigh, LANES), jnp.float32)
+    for l in range(layers):
+        sides_of = sides_of + two_part_dot(errors[l], (wanted_lane == l).astype(jnp.float32))
+    along = iota((chigh, long), 1)
+    coarse_row = jnp.where(along < rows + 64, along // RATIO + 8, 7)
+    side_fix = two_part_dot(
+        sides_of.T, (iota((chigh, long), 0) == coarse_row).astype(jnp.float32)
+    )
+    smooth = []
+    for side in range(2):
+        us = []
+        for l in range(layers):
+            at = 16 * l + 8 * side
+            us.append(su[side, l] + side_fix[at : at + 8])
+        smooth.append((us, strip_sweep(side, us)))
+    fields = list(zip(*smooth))
+    lay_lines(1, [line_rows(l, fields, False) for l in range(layers)])
 
     @pl.loop(1, height // 8 - 1)
     def _(i):
         r = pl.multiple_of(i * 8, 8)
         for l in range(layers):
-            ub[l, pl.ds(r, 8), :] = ub[l, pl.ds(r, 8), :] + spread[l, pl.ds(i + 6, 1), :]
-
-    sweep(ub, into(ua), 1, height // 8 - 1)
-
-    def finish(l, r, new):
-        out[l, pl.ds(r - TOP, 8), :] = new[:, :cols]
-
-    sweep(ua, finish, TOP // 8, (height - TOP) // 8)
+            for p in range(panes):
+                ub[l, p, pl.ds(r, 8), :] = ub[l, p, pl.ds(r, 8), :] + spread[l, p, pl.ds(i + 6, 1), :]
+
+    sweep(ub, into(ua), 1, height // 8 - 1, 1, 0)
+
+    def finish(l, p, r, new):
+        out[l, pl.ds(r - TOP, 8), p * LANES : (p + 1) * LANES] = new
+
+    sweep(ua, finish, TOP // 8, (height - TOP) // 8, 1, 1)
 
     gather_wait(1)
     codes = []
@@ -605,9 +747,9 @@
             v = (1.0 - RELAX) * v + wt * (p + c * around(v))
         die_out[s] = live * v
 
-    wait_all_send(halo_copy)
+    wait_all_send(halo_copy, len(DIRECTIONS))
     for phase in range(2):
-        wait_all_send(lambda k: rough_copy(k, phase))
+        wait_all_send(lambda k: rough_copy(k, phase), N_ROUGH)
 
 
 def per_device(grp_count, tile_count, *args):
@@ -616,7 +758,7 @@
     slots, edge, _ = die_power.shape
     cell = edge // RATIO
     crows = rows // RATIO
-    width, height = cols + LANES, rows + 2 * TOP
+    panes, long, height = cols // LANES, rows + LANES, rows + 2 * TOP
     count = grp_count * tile_count
     n_fields = 2 * layers + 1
     depth = -(-n_fields * HALO // 8) * 8
@@ -627,7 +769,7 @@
     def scratch(*shape):
         return pltpu.VMEM(shape, f32)
 
-    grid = (layers, height, width)
+    grid = (layers, panes, height, LANES)
     return pl.pallas_call(
         functools.partial(kernel, grp_count, tile_count),
         out_shape=(
@@ -637,10 +779,10 @@
         in_specs=[vmem, smem, vmem, vmem, vmem, smem, smem, smem],
         out_specs=(vmem, vmem),
         scratch_shapes=[
-            scratch(n_fields, height, width),
+            scratch(n_fields, panes, height, LANES),
             scratch(*grid),
             scratch(*grid),
-            scratch(layers - 1, height, width),
+            scratch(layers - 1, panes, height, LANES),
             scratch(*grid),
             scratch(*grid),
             scratch(*grid),
@@ -648,10 +790,16 @@
             scratch(rows, LANES),
             scratch(LANES, rows),
             scratch(2, depth, rows),
-            scratch(4, 8, LANES),
+            scratch(3, LANES, LANES),
+            scratch(2, n_fields, 8, long),
+            scratch(2, layers, 8, long),
+            scratch(2, layers, 8, long),
+            scratch(2, layers - 1, 8, long),
+            scratch(2, layers, 8, long),
+            scratch(2, layers, 8, long),
+            scratch(2, height, LANES),
             scratch(rows, cols),
             scratch(rows, LANES),
-            scratch(height, LANES),
             scratch(4, crows, LANES),
             scratch(2, 4, crows, LANES),
             scratch(2, 4, 8, LANES),
@@ -662,10 +810,9 @@
             scratch(cell, LANES),
             scratch(count, cell, LANES),
             scratch(n_fields + 3, crows + 16, LANES),
-            scratch(layers, crows + 16, LANES),
-            scratch(layers, crows + 16, width),
-            pltpu.SemaphoreType.DMA((24,)),
-            pltpu.SemaphoreType.DMA((24,)),
+            scratch(layers, panes, crows + 16, LANES),
+            pltpu.SemaphoreType.DMA((len(DIRECTIONS) + 2 * N_ROUGH,)),
+            pltpu.SemaphoreType.DMA((len(DIRECTIONS) + 2 * N_ROUGH,)),
             pltpu.SemaphoreType.DMA((2, count)),
             pltpu.SemaphoreType.DMA((2, count)),
         ],

time: 77.2 us -> 59.9 us (0.78)
  Pallas kernels: 71.9 us -> 55 us
    pallas_call x1, Pallas kernels: 71.9 us -> 55 us  [per_device(): pl.pallas_call(functools.partial(kernel, grp_count, tile_count), out_shap...]
where the time goes in v1:
time: 59.9 us; the launch traced here: 59.8 us
  Pallas kernels  55 us (92%)
  local copies, waits for them, and re-layouts  4.16 us (7%)
  between operations  0.65 us (1%)
    pallas_call x1, Pallas kernels, per_device(): pl.pallas_call(functools.partial(kernel, grp_count, tile_count), out_shap...  55 us
    unnamed x4, local copies, waits for them, and re-layouts  4.16 us

profile of v1, /device:TPU:0, one launch (start us, length us, event | category | flops | bytes accessed | tf_op | source)
XLA Modules:
  0.0 59.8 jit_solution(16696859084944362853)
XLA Ops:
  0.6 55.0 %shard_map.95 = (f32[6,384,256]{2,1,0:T(8,128)}, f32[6,128,128]{2,1,0:T(8,128)}) custom-call(s32[6,384,256]{2,1,0:T(8,128)} %material.1, f32[8]{0:T(128)} %table.1, f32[384,256]{1,0:T(8,128)} %heat_sink.1, f32[6,384,256]{2,1,0:T(8,128)} %source.1, f32[6,128,128]{2,1,0:T(8,128)} %die_power.1, f32[6]{0:T(128)} %die_conduct.1, f32[6]{0:T(128)} %bond.1, s32[6]{0:T(128)} %place.1), custom_call_target="tpu_custom_call" | custom-call | tf_op jit(solution)/shard_map/pallas_call | solution.py:773
  55.6 0.0 copy-start
  55.6 3.4 %copy.12 = f32[6,384,256]{2,1,0:T(8,128)} copy(f32[6,384,256]{2,1,0:T(8,128)} %get-tuple-element.4) | data formatting | bytes 4718592
  59.0 0.0 copy-done
  59.0 0.7 %copy.13 = f32[6,128,128]{2,1,0:T(8,128)} copy(f32[6,128,128]{2,1,0:T(8,128)S(1)} %copy-done) | data formatting | bytes 786432
Async XLA Ops:
  55.6 3.4 %copy-start = (f32[6,128,128]{2,1,0:T(8,128)S(1)}, f32[6,128,128]{2,1,0:T(8,128)}, u32[]{:S(2)}) copy-start(f32[6,128,128]{2,1,0:T(8,128)} %get-tuple-element.5) | copy-start | bytes 1179652

commit v2 on v1

--- a/solution.py
+++ b/solution.py
@@ -15,9 +15,8 @@
 LANES = 128
 FAR = 1e30
 TINY = 1e-25
-UNROLL = 2
+UNROLL = 5
 MESH = pl.DeviceIdType.MESH
-HIGHEST = lax.Precision.HIGHEST
 DIRECTIONS = ((-1, 0), (1, 0), (0, -1), (0, 1), (-1, -1), (-1, 1), (1, -1), (1, 1), (-1, 0), (1, 0))
 N_ROUGH = 8
 
@@ -33,6 +32,10 @@
 
 def guarded_weight(d):
     return RELAX * inverse(jnp.where(d > TINY, d, 1.0))
+
+
+def unroll_of(n, most=UNROLL):
+    return max(u for u in range(1, most + 1) if n % u == 0)
 
 
 def iota(shape, dim):
@@ -57,17 +60,18 @@
     return merge(y[0], y[1], 0, 1)
 
 
+def halves(a):
+    high = a.astype(jnp.bfloat16)
+    return high, (a - high.astype(jnp.float32)).astype(jnp.bfloat16)
+
+
 def two_part_dot(a, b):
-    high = a.astype(jnp.bfloat16)
-    low = (a - high.astype(jnp.float32)).astype(jnp.bfloat16)
     b = b.astype(jnp.bfloat16)
-    return jnp.dot(high, b, preferred_element_type=jnp.float32) + jnp.dot(
-        low, b, preferred_element_type=jnp.float32
+    return jnp.dot(
+        jnp.concatenate(halves(a), axis=1),
+        jnp.concatenate([b, b], axis=0),
+        preferred_element_type=jnp.float32,
     )
-
-
-def dot(a, b):
-    return jnp.dot(a, b, precision=HIGHEST, preferred_element_type=jnp.float32)
 
 
 def kernel(
@@ -109,9 +113,8 @@
     rough_row,
     rough_corner,
     dies,
-    die_message,
+    fixed,
     all_dies,
-    die_fix,
     all_fixes,
     wide,
     spread,
@@ -136,9 +139,11 @@
     t = lax.axis_index("tile")
     me = g * tile_count + t
 
-    def peer(offset):
-        other = lax.rem(me + offset, count)
-        return other, (other // tile_count, lax.rem(other, tile_count))
+    def each_peer(act):
+        for dg in range(grp_count):
+            for dt in range(tile_count):
+                if dg or dt:
+                    act((lax.rem(g + dg, grp_count), lax.rem(t + dt, tile_count)))
 
     def exists(dy, dx):
         ok = jnp.bool_(True)
@@ -157,6 +162,9 @@
     from_side[:, 0:cut, :] = jnp.full((2, cut, rows), FAR, jnp.float32)
     from_side[:, cut:, :] = jnp.zeros((2, from_side.shape[1] - cut, rows), jnp.float32)
     outer[...] = jnp.where(iota(outer.shape, 2) % 64 < cut, FAR, 0.0)
+    for n in range(2):
+        for at in (0, edge + 8):
+            dies[n, :, pl.ds(at, 8), :] = jnp.zeros((slots, 8, edge), jnp.float32)
     rough_side[...] = jnp.zeros_like(rough_side)
     rough_row[...] = jnp.zeros_like(rough_row)
     rough_corner[...] = jnp.zeros_like(rough_corner)
@@ -164,9 +172,9 @@
 
     barrier = pltpu.get_barrier_semaphore()
 
-    @pl.loop(1, count)
-    def _(offset):
-        pl.semaphore_signal(barrier, inc=1, device_id=peer(offset)[1], device_id_type=MESH)
+    each_peer(
+        lambda where: pl.semaphore_signal(barrier, inc=1, device_id=where, device_id_type=MESH)
+    )
 
     lane8 = iota((8, LANES), 1)
     sub8 = iota((8, LANES), 0)
@@ -179,7 +187,7 @@
 
     doubled = [jnp.full((8, LANES), 2.0 * table[m], jnp.float32) for m in range(table.shape[0])]
 
-    @pl.loop(0, rows // 8)
+    @pl.loop(0, rows // 8, unroll=unroll_of(rows // 8, 4))
     def _(i):
         r = pl.multiple_of(i * 8, 8)
         edges = jnp.zeros((8, LANES), jnp.float32)
@@ -269,67 +277,73 @@
 
     start_all(halo_copy, len(DIRECTIONS))
 
-    srow, scol = iota((edge, edge), 0), iota((edge, edge), 1)
+    col_d = iota((8, LANES), 1)
     one, none = jnp.float32(1.0), jnp.float32(0.0)
-    sides = (
-        jnp.where(srow > 0, one, none) + jnp.where(srow < edge - 1, one, none)
-        + jnp.where(scol > 0, one, none) + jnp.where(scol < edge - 1, one, none)
-    )
-
-    def around(v):
+    inner = jnp.where(col_d > 0, one, none) + jnp.where(col_d < edge - 1, one, none) + 1.0
+    first_row = jnp.where(sub8 > 0, one, none)
+    last_row = jnp.where(sub8 < 7, one, none)
+    beside = (
+        jnp.abs(iota((edge, edge), 0) - iota((edge, edge), 1)) == 1
+    ).astype(jnp.float32)
+    body = pl.ds(8, edge)
+    tall = edge // 8
+
+    def die_diagonal(c, b):
+        tops = [c * (inner + first_row) + b, c * (inner + 1.0) + b, c * (inner + last_row) + b]
+        ws = [guarded_weight(d) for d in tops]
+
+        def full(x):
+            return jnp.concatenate([x[0]] + [x[1]] * (tall - 2) + [x[2]], axis=0)
+
+        return full(tops), full(ws)
+
+    def around(n, s):
+        v = dies[n, s, body, :]
         return (
-            jnp.where(srow > 0, shift(v, 1, 0), 0.0)
-            + jnp.where(srow < edge - 1, shift(v, -1, 0), 0.0)
-            + jnp.where(scol > 0, shift(v, 1, 1), 0.0)
-            + jnp.where(scol < edge - 1, shift(v, -1, 1), 0.0)
-        )
-
-    rows_in = (iota((cell, edge), 0) == iota((cell, edge), 1) // RATIO).astype(jnp.float32)
+            dies[n, s, pl.ds(7, edge), :] + dies[n, s, pl.ds(9, edge), :] + two_part_dot(v, beside)
+        )
+
+    rows_in = (iota((cell, edge), 0) == iota((cell, edge), 1) // RATIO).astype(jnp.bfloat16)
+    rows_in = jnp.concatenate([rows_in, rows_in], axis=1)
     message = jnp.zeros((cell, LANES), jnp.float32)
-    row_m = iota((8, LANES), 0)
     params = jnp.full((8, LANES), -1.0, jnp.float32)
     for s in range(slots):
         c, b = die_conduct[s], bond[s]
         live = jnp.where(place[s] >= 0, 1.0, 0.0)
         p = die_power[s]
-        d = c * sides + b
-        wt = guarded_weight(d)
-        v = wt * p
-        v = (1.0 - RELAX) * v + wt * (p + c * around(v))
-        dies[s] = v
-        resid = live * (p + c * around(v) - d * v)
+        d, wt = die_diagonal(c, b)
+        dies[0, s, body, :] = wt * p
+        dies[1, s, body, :] = (1.0 - RELAX) * dies[0, s, body, :] + wt * (p + c * around(0, s))
+        resid = p + c * around(1, s) - d * dies[1, s, body, :]
         cols_in = (
             iota((edge, LANES), 0) // RATIO + cell * s == iota((edge, LANES), 1)
         ).astype(jnp.float32)
-        message = message + dot(dot(rows_in, resid), cols_in)
+        by_row = jnp.dot(
+            rows_in, jnp.concatenate(halves(resid), axis=0), preferred_element_type=jnp.float32
+        )
+        message = message + live * two_part_dot(by_row, cols_in)
         mine = lane8 // cell == s
         value = jnp.where(
-            row_m == 0, c, jnp.where(row_m == 1, b * area, place[s].astype(jnp.float32))
+            sub8 == 0, c, jnp.where(sub8 == 1, b * area, place[s].astype(jnp.float32))
         )
         params = jnp.where(mine, value, params)
-    die_message[0:cell, :] = message
-    die_message[cell : cell + 8, :] = params
-    all_dies[me] = die_message[...]
-
-    def gather_copy(phase, other, slot, where):
-        src, dst = (die_message, all_dies) if phase == 0 else (die_fix, all_fixes)
-        return pltpu.make_async_remote_copy(
-            src_ref=src, dst_ref=dst.at[slot],
-            send_sem=gather_send.at[phase, other], recv_sem=gather_recv.at[phase, slot],
-            device_id=where, device_id_type=MESH,
-        )
+    all_dies[me, 0:cell, :] = message
+    all_dies[me, cell : cell + 8, :] = params
 
     def gather_start(phase):
-        @pl.loop(1, count)
-        def _(offset):
-            other, where = peer(offset)
-            gather_copy(phase, other, me, where).start()
+        every = (all_dies, all_fixes)[phase]
+        each_peer(
+            lambda where: pltpu.make_async_remote_copy(
+                src_ref=every.at[me], dst_ref=every.at[me],
+                send_sem=gather_send.at[phase], recv_sem=gather_recv.at[phase],
+                device_id=where, device_id_type=MESH,
+            ).start()
+        )
 
     def gather_wait(phase):
-        @pl.loop(1, count)
-        def _(offset):
-            other, where = peer(offset)
-            gather_copy(phase, other, other, where).wait()
+        others = (all_dies, all_fixes)[phase].at[pl.ds(0, count - 1)]
+        for sem in (gather_send, gather_recv):
+            pltpu.make_async_copy(others, others, sem.at[phase]).wait()
 
     gather_start(0)
 
@@ -447,7 +461,7 @@
     def line_ends(line, l, q):
         return shift(line, -(8 * l + 2 * q + 1), 1)
 
-    @pl.loop(1, height // 8 - 1, unroll=UNROLL)
+    @pl.loop(1, height // 8 - 1, unroll=unroll_of(height // 8 - 2))
     def _(i):
         r = pl.multiple_of(i * 8, 8)
         here = pl.ds(r, 8)
@@ -502,7 +516,7 @@
         return [[u[l, p, pl.ds(r, 8), :] for p in range(panes)] for l in range(layers)]
 
     def sweep(u, store, first, last, k, q):
-        @pl.loop(first, last, unroll=UNROLL)
+        @pl.loop(first, last, unroll=unroll_of(last - first))
         def _(i):
             r = pl.multiple_of(i * 8, 8)
             us = layers_at(u, r)
@@ -523,7 +537,7 @@
 
     sweep(ua, into(ub), 1, height // 8 - 1, 0, 1)
 
-    @pl.loop(0, crows, unroll=UNROLL)
+    @pl.loop(0, crows, unroll=unroll_of(crows))
     def _(i):
         r = pl.multiple_of(i * 8 + TOP, 8)
         us = layers_at(ub, r)
@@ -556,13 +570,14 @@
 
         def add(d, acc, lo=lo):
             block = all_dies[d]
-            where = block[cell + 2 : cell + 3, :]
+            where = all_dies[d, pl.ds(cell + 2, 1), :]
             return tuple(
-                a + jnp.where(where == wanted[lo + j], block, 0.0) for j, a in enumerate(acc)
+                jnp.where(where == wanted[lo + j], block, a) for j, a in enumerate(acc)
             )
 
         acc = lax.fori_loop(
-            0, count, add, tuple(jnp.zeros((parts, LANES), jnp.float32) for _ in range(across + 2))
+            0, count, add, tuple(jnp.zeros((parts, LANES), jnp.float32) for _ in range(across + 2)),
+            unroll=unroll_of(count, 8),
         )
         lane_p = iota((parts, LANES), 1)
         line = jnp.zeros((parts, LANES), jnp.float32)
@@ -666,8 +681,7 @@
     for a in range(down):
         piece = shift(top[8 + a * cell : 8 + (a + 1) * cell], a * ccols - 8, 1)
         fix = jnp.where(lane_c // ccols == a, piece, fix)
-    die_fix[...] = fix
-    all_fixes[me] = die_fix[...]
+    all_fixes[me] = fix
     gather_start(1)
 
     pick = (iota((LANES, cols), 0) == 8 + iota((LANES, cols), 1) // RATIO).astype(jnp.float32)
@@ -713,27 +727,14 @@
     sweep(ua, finish, TOP // 8, (height - TOP) // 8, 1, 1)
 
     gather_wait(1)
-    codes = []
+    group = lane_c // cell
+    cols_out = (iota((LANES, edge), 0) == iota((LANES, edge), 1) // RATIO).astype(jnp.float32)
     for s in range(slots):
         spot = jnp.maximum(place[s], 0)
         pr, pc = spot // span, lax.rem(spot, span)
         target = (pr // down) * tile_count + pc // across
         local = lax.rem(pr, down) * across + lax.rem(pc, across)
-        codes.append(jnp.where(place[s] >= 0, target * 8 + local, -1))
-    group = lane_c // cell
-
-    def collect(d, acc):
-        block = all_fixes[d]
-        code = group + d * 8
-        return tuple(a + jnp.where(code == codes[s], block, 0.0) for s, a in enumerate(acc))
-
-    fixes = lax.fori_loop(
-        0, count, collect, tuple(jnp.zeros((cell, LANES), jnp.float32) for _ in range(slots))
-    )
-    rows_out = (iota((edge, cell), 0) // RATIO == iota((edge, cell), 1)).astype(jnp.float32)
-    cols_out = (iota((LANES, edge), 0) == iota((LANES, edge), 1) // RATIO).astype(jnp.float32)
-    for s in range(slots):
-        x = fixes[s]
+        x = jnp.where(group == local, all_fixes[target], 0.0)
         step = LANES // 2
         while step >= cell:
             x = x + shift(x, step, 1)
@@ -741,10 +742,16 @@
         c, b = die_conduct[s], bond[s]
         live = jnp.where(place[s] >= 0, 1.0, 0.0)
         p = die_power[s]
-        wt = guarded_weight(c * sides + b)
-        v = dies[s] + live * dot(rows_out, dot(x, cols_out))
-        for _ in range(NU):
-            v = (1.0 - RELAX) * v + wt * (p + c * around(v))
+        wt = die_diagonal(c, b)[1]
+        fixed[s] = live * two_part_dot(x, cols_out)
+        for k in range(tall):
+            dies[0, s, pl.ds(8 + 8 * k, 8), :] = (
+                dies[1, s, pl.ds(8 + 8 * k, 8), :] + fixed[s, pl.ds(k, 1), :]
+            )
+        for n in range(NU):
+            v = (1.0 - RELAX) * dies[n % 2, s, body, :] + wt * (p + c * around(n % 2, s))
+            if n < NU - 1:
+                dies[(n + 1) % 2, s, body, :] = v
         die_out[s] = live * v
 
     wait_all_send(halo_copy, len(DIRECTIONS))
@@ -804,17 +811,16 @@
             scratch(2, 4, crows, LANES),
             scratch(2, 4, 8, LANES),
             scratch(4, 4, 8, LANES),
-            scratch(slots, edge, edge),
-            scratch(cell + 8, LANES),
+            scratch(2, slots, edge + 16, edge),
+            scratch(slots, cell, edge),
             scratch(count, cell + 8, LANES),
-            scratch(cell, LANES),
             scratch(count, cell, LANES),
             scratch(n_fields + 3, crows + 16, LANES),
             scratch(layers, panes, crows + 16, LANES),
             pltpu.SemaphoreType.DMA((len(DIRECTIONS) + 2 * N_ROUGH,)),
             pltpu.SemaphoreType.DMA((len(DIRECTIONS) + 2 * N_ROUGH,)),
-            pltpu.SemaphoreType.DMA((2, count)),
-            pltpu.SemaphoreType.DMA((2, count)),
+            pltpu.SemaphoreType.DMA((2,)),
+            pltpu.SemaphoreType.DMA((2,)),
         ],
         compiler_params=pltpu.CompilerParams(
             collective_id=0, has_side_effects=True, vmem_limit_bytes=60 * 1024 * 1024

time: 59.9 us -> 50.1 us (0.84)
  Pallas kernels: 55 us -> 45.1 us
    pallas_call x1, Pallas kernels: 55 us -> 45.1 us  [per_device(): pl.pallas_call(functools.partial(kernel, grp_count, tile_count), out_shap...]
where the time goes in v2:
time: 50.1 us; the launch traced here: 49.9 us
  Pallas kernels  45.1 us (90%)
  local copies, waits for them, and re-layouts  4.16 us (8%)
  between operations  0.65 us (1%)
    pallas_call x1, Pallas kernels, per_device(): pl.pallas_call(functools.partial(kernel, grp_count, tile_count), out_shap...  45.1 us
    unnamed x4, local copies, waits for them, and re-layouts  4.16 us

profile of v2, /device:TPU:0, one launch (start us, length us, event | category | flops | bytes accessed | tf_op | source)
XLA Modules:
  0.0 49.9 jit_solution(15442195206113355902)
XLA Ops:
  0.6 45.1 %shard_map.95 = (f32[6,384,256]{2,1,0:T(8,128)}, f32[6,128,128]{2,1,0:T(8,128)}) custom-call(s32[6,384,256]{2,1,0:T(8,128)} %material.1, f32[8]{0:T(128)} %table.1, f32[384,256]{1,0:T(8,128)} %heat_sink.1, f32[6,384,256]{2,1,0:T(8,128)} %source.1, f32[6,128,128]{2,1,0:T(8,128)} %die_power.1, f32[6]{0:T(128)} %die_conduct.1, f32[6]{0:T(128)} %bond.1, s32[6]{0:T(128)} %place.1), custom_call_target="tpu_custom_call" | custom-call | tf_op jit(solution)/shard_map/pallas_call | solution.py:780
  45.8 0.0 copy-start
  45.8 3.4 %copy.12 = f32[6,384,256]{2,1,0:T(8,128)} copy(f32[6,384,256]{2,1,0:T(8,128)} %get-tuple-element.4) | data formatting | bytes 4718592
  49.2 0.0 copy-done
  49.2 0.7 %copy.13 = f32[6,128,128]{2,1,0:T(8,128)} copy(f32[6,128,128]{2,1,0:T(8,128)S(1)} %copy-done) | data formatting | bytes 786432
Async XLA Ops:
  45.8 3.4 %copy-start = (f32[6,128,128]{2,1,0:T(8,128)S(1)}, f32[6,128,128]{2,1,0:T(8,128)}, u32[]{:S(2)}) copy-start(f32[6,128,128]{2,1,0:T(8,128)} %get-tuple-element.5) | copy-start | bytes 1179652

commit v3 on v2

--- a/solution.py
+++ b/solution.py
@@ -77,16 +77,20 @@
 def kernel(
     grp_count,
     tile_count,
-    material,
+    material_far,
     table,
-    heat_sink,
-    source,
-    die_power,
+    heat_sink_far,
+    source_far,
+    die_power_far,
     die_conduct,
     bond,
     place,
     out,
     die_out,
+    material,
+    heat_sink,
+    source,
+    die_power,
     field,
     zx,
     zy,
@@ -122,6 +126,8 @@
     recv_sem,
     gather_send,
     gather_recv,
+    load_sem,
+    die_sem,
 ):
     layers, rows, cols = material.shape
     slots, edge, _ = die_power.shape
@@ -153,6 +159,26 @@
             ok = jnp.logical_and(ok, t > 0 if dx < 0 else t < tile_count - 1)
         return ok
 
+    pieces = unroll_of(rows // 8, 4)
+    piece = rows // pieces
+
+    def loads(n):
+        some = pl.ds(pl.multiple_of(n * piece, 8), piece)
+        pairs = (
+            (material_far.at[:, some, :], material.at[:, some, :]),
+            (source_far.at[:, some, :], source.at[:, some, :]),
+            (heat_sink_far.at[some, :], heat_sink.at[some, :]),
+        )
+        return [
+            pltpu.make_async_copy(a, b, load_sem.at[j, n]) for j, (a, b) in enumerate(pairs)
+        ]
+
+    die_load = pltpu.make_async_copy(die_power_far, die_power, die_sem)
+    for n in range(pieces):
+        for load in loads(n):
+            load.start()
+    die_load.start()
+
     for top in (0, height - TOP):
         field[0:layers, :, top : top + TOP, :] = jnp.full((layers, panes, TOP, LANES), FAR, jnp.float32)
         field[layers:n_fields, :, top : top + TOP, :] = jnp.zeros(
@@ -187,43 +213,48 @@
 
     doubled = [jnp.full((8, LANES), 2.0 * table[m], jnp.float32) for m in range(table.shape[0])]
 
-    @pl.loop(0, rows // 8, unroll=unroll_of(rows // 8, 4))
-    def _(i):
-        r = pl.multiple_of(i * 8, 8)
-        edges = jnp.zeros((8, LANES), jnp.float32)
-        summed = [[] for _ in range(panes)]
-        for f in range(n_fields):
-            xs = []
+    @pl.loop(0, pieces)
+    def _(n):
+        for load in loads(n):
+            load.wait()
+
+        @pl.loop(0, piece // 8, unroll=unroll_of(piece // 8, 4))
+        def _(i):
+            r = pl.multiple_of(n * piece + i * 8, 8)
+            edges = jnp.zeros((8, LANES), jnp.float32)
+            summed = [[] for _ in range(panes)]
+            for f in range(n_fields):
+                xs = []
+                for p in range(panes):
+                    part = slice(p * LANES, (p + 1) * LANES)
+                    if f < layers:
+                        kind = material[f, pl.ds(r, 8), part]
+                        values = list(doubled)
+                        bit = 1
+                        while len(values) > 1:
+                            odd = (kind & bit) != 0
+                            values = [
+                                jnp.where(odd, values[m + 1], values[m]) if m + 1 < len(values) else values[m]
+                                for m in range(0, len(values), 2)
+                            ]
+                            bit *= 2
+                        summed[p].append(values[0])
+                        x = inverse(values[0])
+                    elif f < 2 * layers:
+                        x = source[f - layers, pl.ds(r, 8), part]
+                    else:
+                        x = heat_sink[pl.ds(r, 8), part]
+                        summed[p].append(x)
+                    field[f, p, pl.ds(TOP + r, 8), :] = x
+                    xs.append(x)
+                a, b = right_lane(f), left_lane(f)
+                right = shift(xs[-1], HALO + a, 1)
+                left = shift(xs[0], b, 1)
+                edges = jnp.where((lane8 >= a) & (lane8 < a + HALO), right, edges)
+                edges = jnp.where((lane8 >= b) & (lane8 < b + HALO), left, edges)
+            packed[pl.ds(r, 8), :] = edges
             for p in range(panes):
-                part = slice(p * LANES, (p + 1) * LANES)
-                if f < layers:
-                    kind = material[f, pl.ds(r, 8), part]
-                    values = list(doubled)
-                    bit = 1
-                    while len(values) > 1:
-                        odd = (kind & bit) != 0
-                        values = [
-                            jnp.where(odd, values[m + 1], values[m]) if m + 1 < len(values) else values[m]
-                            for m in range(0, len(values), 2)
-                        ]
-                        bit *= 2
-                    summed[p].append(values[0])
-                    x = inverse(values[0])
-                elif f < 2 * layers:
-                    x = source[f - layers, pl.ds(r, 8), part]
-                else:
-                    x = heat_sink[pl.ds(r, 8), part]
-                    summed[p].append(x)
-                field[f, p, pl.ds(TOP + r, 8), :] = x
-                xs.append(x)
-            a, b = right_lane(f), left_lane(f)
-            right = shift(xs[-1], HALO + a, 1)
-            left = shift(xs[0], b, 1)
-            edges = jnp.where((lane8 >= a) & (lane8 < a + HALO), right, edges)
-            edges = jnp.where((lane8 >= b) & (lane8 < b + HALO), left, edges)
-        packed[pl.ds(r, 8), :] = edges
-        for p in range(panes):
-            sums[pl.ds(r, 8), p * LANES : (p + 1) * LANES] = row_sums(summed[p])
+                sums[pl.ds(r, 8), p * LANES : (p + 1) * LANES] = row_sums(summed[p])
 
     turned[...] = packed[...].T
 
@@ -277,6 +308,64 @@
 
     start_all(halo_copy, len(DIRECTIONS))
 
+    first8, last8 = lane8 == 0, lane8 == LANES - 1
+
+    def from_right(xs, p, end):
+        turn = shift(xs[p], -1, 1)
+        if p < panes - 1:
+            return jnp.where(last8, shift(xs[p + 1], -1, 1), turn)
+        return turn if end is None else jnp.where(last8, end, turn)
+
+    def from_left(xs, p, end):
+        return jnp.where(first8, end if p == 0 else shift(xs[p - 1], 1, 1), shift(xs[p], 1, 1))
+
+    def line_ends(line, l, q):
+        return shift(line, -(8 * l + 2 * q + 1), 1)
+
+    early, late = TOP // 8 + 2, (height - TOP) // 8 - 1
+
+    def across_down(r, l, p):
+        fx = inverse(field[l, p, pl.ds(r, 8), :] + field[l, p, pl.ds(r + 1, 8), :])
+        zx[l, p, pl.ds(r, 8), :] = fx
+        return fx
+
+    def faces(i, line):
+        r = pl.multiple_of(i * 8, 8)
+        here = pl.ds(r, 8)
+        ks = [[field[l, p, here, :] for p in range(panes)] for l in range(layers)]
+        fxs = [[across_down(r, l, p) for p in range(panes)] for l in range(layers)]
+        below = [None] * panes
+        for l in range(layers):
+            k = ks[l]
+            ends = 0.0 if line is None else line_ends(line, l, 0)
+            fys = [inverse(k[p] + from_right(k, p, None)) for p in range(panes)]
+            fys[-1] = jnp.where(last8, ends, fys[-1])
+            for p in range(panes):
+                fy = fys[p]
+                zy[l, p, here, :] = fy
+                d = fxs[l][p] + zx[l, p, pl.ds(r - 1, 8), :] + fy + from_left(fys, p, ends)
+                d = d + (field[2 * layers, p, here, :] if l == 0 else below[p])
+                if l < layers - 1:
+                    below[p] = inverse(k[p] + ks[l + 1][p])
+                    zz[l, p, here, :] = below[p]
+                    d = d + below[p]
+                diag[l, p, here, :] = d
+                if line is not None:
+                    first_sweep(here, l, p, d)
+
+    def first_sweep(here, l, p, d):
+        wt = guarded_weight(d)
+        weight[l, p, here, :] = wt
+        ua[l, p, here, :] = wt * field[layers + l, p, here, :]
+
+    for l in range(layers):
+        for p in range(panes):
+            across_down((early - 1) * 8, l, p)
+
+    @pl.loop(early, late, unroll=unroll_of(late - early))
+    def _(i):
+        faces(i, None)
+
     col_d = iota((8, LANES), 1)
     one, none = jnp.float32(1.0), jnp.float32(0.0)
     inner = jnp.where(col_d > 0, one, none) + jnp.where(col_d < edge - 1, one, none) + 1.0
@@ -306,6 +395,7 @@
     rows_in = (iota((cell, edge), 0) == iota((cell, edge), 1) // RATIO).astype(jnp.bfloat16)
     rows_in = jnp.concatenate([rows_in, rows_in], axis=1)
     message = jnp.zeros((cell, LANES), jnp.float32)
+    die_load.wait()
     params = jnp.full((8, LANES), -1.0, jnp.float32)
     for s in range(slots):
         c, b = die_conduct[s], bond[s]
@@ -345,8 +435,6 @@
         for sem in (gather_send, gather_recv):
             pltpu.make_async_copy(others, others, sem.at[phase]).wait()
 
-    gather_start(0)
-
     def gathered(total, first_tile):
         pick = (iota((cols, LANES), 0) // RATIO == iota((cols, LANES), 1)).astype(jnp.float32)
         folded[...] = two_part_dot(sums[...], pick)
@@ -359,9 +447,10 @@
             rough[first_tile + tile] = result
 
     gathered(layers + 1, 0)
+
+    wait_all_recv(halo_copy, len(DIRECTIONS))
+    gather_start(0)
     start_all(lambda k: rough_copy(k, 0), N_ROUGH)
-
-    wait_all_recv(halo_copy, len(DIRECTIONS))
     extra = [outer[j].T for j in range(3)]
 
     def woven(near, far, f, first):
@@ -447,52 +536,29 @@
     fields = list(zip(*smooth))
     lay_lines(0, [line_rows(l, fields, True) for l in range(layers)])
 
-    first8, last8 = lane8 == 0, lane8 == LANES - 1
-
-    def from_right(xs, p, end):
-        turn = shift(xs[p], -1, 1)
-        if p < panes - 1:
-            return jnp.where(last8, shift(xs[p + 1], -1, 1), turn)
-        return turn if end is None else jnp.where(last8, end, turn)
-
-    def from_left(xs, p, end):
-        return jnp.where(first8, end if p == 0 else shift(xs[p - 1], 1, 1), shift(xs[p], 1, 1))
-
-    def line_ends(line, l, q):
-        return shift(line, -(8 * l + 2 * q + 1), 1)
-
-    @pl.loop(1, height // 8 - 1, unroll=unroll_of(height // 8 - 2))
+    def whole(i):
+        faces(i, lines[0, pl.ds(pl.multiple_of(i * 8, 8), 8), :])
+
+    pl.loop(1, early, unroll=early - 1)(whole)
+
+    @pl.loop(early, late, unroll=unroll_of(late - early))
     def _(i):
-        r = pl.multiple_of(i * 8, 8)
-        here = pl.ds(r, 8)
+        here = pl.ds(pl.multiple_of(i * 8, 8), 8)
         line = lines[0, here, :]
-        ks = [[field[l, p, here, :] for p in range(panes)] for l in range(layers)]
-        fxs = []
         for l in range(layers):
-            fxs.append([])
+            ends = line_ends(line, l, 0)
+            zy[l, panes - 1, here, :] = jnp.where(last8, ends, zy[l, panes - 1, here, :])
             for p in range(panes):
-                fx = inverse(ks[l][p] + field[l, p, pl.ds(r + 1, 8), :])
-                zx[l, p, here, :] = fx
-                fxs[l].append(fx)
-        below = [None] * panes
-        for l in range(layers):
-            k = ks[l]
-            ends = line_ends(line, l, 0)
-            fys = [inverse(k[p] + from_right(k, p, None)) for p in range(panes)]
-            fys[-1] = jnp.where(last8, ends, fys[-1])
-            for p in range(panes):
-                fy = fys[p]
-                zy[l, p, here, :] = fy
-                d = fxs[l][p] + zx[l, p, pl.ds(r - 1, 8), :] + fy + from_left(fys, p, ends)
-                d = d + (field[2 * layers, p, here, :] if l == 0 else below[p])
-                if l < layers - 1:
-                    below[p] = inverse(k[p] + ks[l + 1][p])
-                    zz[l, p, here, :] = below[p]
-                    d = d + below[p]
-                diag[l, p, here, :] = d
-                wt = guarded_weight(d)
-                weight[l, p, here, :] = wt
-                ua[l, p, here, :] = wt * field[layers + l, p, here, :]
+                d = diag[l, p, here, :]
+                if p == 0:
+                    d = d + jnp.where(first8, ends, 0.0)
+                if p == panes - 1:
+                    d = d + jnp.where(last8, ends, 0.0)
+                if p in (0, panes - 1):
+                    diag[l, p, here, :] = d
+                first_sweep(here, l, p, d)
+
+    pl.loop(late, height // 8 - 1, unroll=height // 8 - 1 - late)(whole)
 
     def pulled(u, r, l, us, line, q):
         here = pl.ds(r, 8)
@@ -555,9 +621,51 @@
     gathered(layers, 2)
     start_all(lambda k: rough_copy(k, 1), N_ROUGH)
 
+    chigh = crows + 16
+
+    def join(phase):
+        wait_all_recv(lambda k: rough_copy(k, phase), N_ROUGH)
+        for f in range(layers + 1 if phase == 0 else layers):
+            tile, q = 2 * phase + f // per, f % per
+            target = f if phase == 0 else layers + 1 + f
+
+            def joined(left, middle, right, size):
+                lane = iota((size, LANES), 1)
+                x = shift(middle, 8 - ccols * q, 1)
+                x = jnp.where((lane >= 8) & (lane < 8 + ccols), x, 0.0)
+                x = jnp.where(lane < 8, shift(left, 8 - ccols - ccols * q, 1), x)
+                return jnp.where(
+                    (lane >= 8 + ccols) & (lane < 16 + ccols),
+                    shift(right, 8 + ccols - ccols * q, 1),
+                    x,
+                )
+
+            wide[target, 8 : 8 + crows, :] = joined(
+                rough_side[1, tile], rough[tile], rough_side[0, tile], crows
+            )
+            wide[target, 0:8, :] = joined(
+                rough_corner[3, tile], rough_row[1, tile], rough_corner[2, tile], 8
+            )
+            wide[target, 8 + crows : chigh, :] = joined(
+                rough_corner[1, tile], rough_row[0, tile], rough_corner[0, tile], 8
+            )
+
+    join(0)
+    kc = [wide[l] * (0.5 / area) for l in range(layers)]
+    cx = [harmonic(k, shift(k, -1, 0)) for k in kc]
+    cy = [harmonic(k, shift(k, -1, 1)) for k in kc]
+    cz = [harmonic(kc[l], kc[l + 1]) * area for l in range(layers - 1)]
+    sums_of = []
+    for l in range(layers):
+        d = cx[l] + shift(cx[l], 1, 0) + cy[l] + shift(cy[l], 1, 1)
+        if l == 0:
+            d = d + wide[layers]
+        else:
+            d = d + cz[l - 1]
+        sums_of.append(d + cz[l] if l < layers - 1 else d)
+
     gather_wait(0)
     span = tile_count * across
-    chigh = crows + 16
     parts = cell + 8
     spots = [(a, b) for a in range(-1, down + 1) for b in range(-1, across + 1)]
     wanted = []
@@ -605,47 +713,8 @@
             line[cell + 1 : cell + 2], (size, LANES)
         )
 
-    for phase in range(2):
-        wait_all_recv(lambda k: rough_copy(k, phase), N_ROUGH)
-        for f in range(layers + 1 if phase == 0 else layers):
-            tile, q = 2 * phase + f // per, f % per
-            target = f if phase == 0 else layers + 1 + f
-
-            def joined(left, middle, right, size):
-                lane = iota((size, LANES), 1)
-                x = shift(middle, 8 - ccols * q, 1)
-                x = jnp.where((lane >= 8) & (lane < 8 + ccols), x, 0.0)
-                x = jnp.where(lane < 8, shift(left, 8 - ccols - ccols * q, 1), x)
-                return jnp.where(
-                    (lane >= 8 + ccols) & (lane < 16 + ccols),
-                    shift(right, 8 + ccols - ccols * q, 1),
-                    x,
-                )
-
-            wide[target, 8 : 8 + crows, :] = joined(
-                rough_side[1, tile], rough[tile], rough_side[0, tile], crows
-            )
-            wide[target, 0:8, :] = joined(
-                rough_corner[3, tile], rough_row[1, tile], rough_corner[2, tile], 8
-            )
-            wide[target, 8 + crows : chigh, :] = joined(
-                rough_corner[1, tile], rough_row[0, tile], rough_corner[0, tile], 8
-            )
-
-    kc = [wide[l] * (0.5 / area) for l in range(layers)]
-    cx = [harmonic(k, shift(k, -1, 0)) for k in kc]
-    cy = [harmonic(k, shift(k, -1, 1)) for k in kc]
-    cz = [harmonic(kc[l], kc[l + 1]) * area for l in range(layers - 1)]
     top_rhs, top_c, top_b = (wide[2 * layers + 1 + j] for j in range(3))
-    weights = []
-    for l in range(layers):
-        d = cx[l] + shift(cx[l], 1, 0) + cy[l] + shift(cy[l], 1, 1)
-        if l == 0:
-            d = d + wide[layers]
-        else:
-            d = d + cz[l - 1]
-        d = d + (cz[l] if l < layers - 1 else top_b)
-        weights.append(guarded_weight(d))
+    weights = [guarded_weight(d) for d in sums_of[:-1]] + [guarded_weight(sums_of[-1] + top_b)]
     crow = (iota((chigh, LANES), 0) + (cell - 8)) % cell
     ccol = (iota((chigh, LANES), 1) + (cell - 8)) % cell
     low_x, high_x = crow != 0, crow != cell - 1
@@ -653,6 +722,7 @@
     near = sum(jnp.where(m, one, none) for m in (low_x, high_x, low_y, high_y))
     top_d = top_c * near + top_b
     top_w = guarded_weight(top_d)
+    join(1)
     errors = [weights[l] * wide[layers + 1 + l] for l in range(layers)]
     top = top_w * top_rhs
     for _ in range(NC - 1):
@@ -771,6 +841,7 @@
     depth = -(-n_fields * HALO // 8) * 8
     vmem = pl.BlockSpec(memory_space=pltpu.VMEM)
     smem = pl.BlockSpec(memory_space=pltpu.SMEM)
+    far = pl.BlockSpec(memory_space=pl.ANY)
     f32 = jnp.float32
 
     def scratch(*shape):
@@ -780,12 +851,16 @@
     return pl.pallas_call(
         functools.partial(kernel, grp_count, tile_count),
         out_shape=(
-            jax.ShapeDtypeStruct((layers, rows, cols), f32),
-            jax.ShapeDtypeStruct((slots, edge, edge), f32),
+            pltpu.VMEM((layers, rows, cols), f32),
+            pltpu.VMEM((slots, edge, edge), f32),
         ),
-        in_specs=[vmem, smem, vmem, vmem, vmem, smem, smem, smem],
+        in_specs=[far, smem, far, far, far, smem, smem, smem],
         out_specs=(vmem, vmem),
         scratch_shapes=[
+            pltpu.VMEM(material.shape, material.dtype),
+            scratch(rows, cols),
+            scratch(layers, rows, cols),
+            scratch(slots, edge, edge),
             scratch(n_fields, panes, height, LANES),
             scratch(*grid),
             scratch(*grid),
@@ -821,6 +896,8 @@
             pltpu.SemaphoreType.DMA((len(DIRECTIONS) + 2 * N_ROUGH,)),
             pltpu.SemaphoreType.DMA((2,)),
             pltpu.SemaphoreType.DMA((2,)),
+            pltpu.SemaphoreType.DMA((3, unroll_of(rows // 8, 4))),
+            pltpu.SemaphoreType.DMA,
         ],
         compiler_params=pltpu.CompilerParams(
             collective_id=0, has_side_effects=True, vmem_limit_bytes=60 * 1024 * 1024

time: 50.1 us -> 42 us (0.84)
  Pallas kernels: 45.1 us -> 39 us
  local copies, waits for them, and re-layouts: 4.16 us -> 2.15 us
    pallas_call x1, Pallas kernels: 45.1 us -> 39 us  [per_device(): pl.pallas_call(functools.partial(kernel, grp_count, tile_count), out_shap...]
    unnamed x4 -> x2, local copies, waits for them, and re-layouts: 4.16 us -> 2.15 us
where the time goes in v3:
time: 42 us; the launch traced here: 41.8 us
  Pallas kernels  39 us (93%)
  local copies, waits for them, and re-layouts  2.15 us (5%)
  between operations  0.64 us (2%)
    pallas_call x1, Pallas kernels, per_device(): pl.pallas_call(functools.partial(kernel, grp_count, tile_count), out_shap...  39 us
    unnamed x2, local copies, waits for them, and re-layouts  2.15 us

profile of v3, /device:TPU:0, one launch (start us, length us, event | category | flops | bytes accessed | tf_op | source)
XLA Modules:
  0.0 41.8 jit_solution(16706784995713936993)
XLA Ops:
  0.6 39.0 %shard_map.95 = (f32[6,384,256]{2,1,0:T(8,128)S(1)}, f32[6,128,128]{2,1,0:T(8,128)S(1)}) custom-call(s32[6,384,256]{2,1,0:T(8,128)} %material_far.1, f32[8]{0:T(128)} %table.1, f32[384,256]{1,0:T(8,128)} %heat_sink_far.1, f32[6,384,256]{2,1,0:T(8,128)} %source_far.1, f32[6,128,128]{2,1,0:T(8,128)} %die_power_far.1, f32[6]{0:T(128)} %die_conduct.1, f32[6]{0:T(128)} %bond.1, ...), custom_call_target="tpu_custom_call" | custom-call | tf_op jit(solution)/shard_map/pallas_call | solution.py:851
  39.6 1.4 %copy.12 = f32[6,384,256]{2,1,0:T(8,128)} copy(f32[6,384,256]{2,1,0:T(8,128)S(1)} %get-tuple-element.2) | data formatting | bytes 4718592
  41.0 0.7 %copy.13 = f32[6,128,128]{2,1,0:T(8,128)} copy(f32[6,128,128]{2,1,0:T(8,128)S(1)} %get-tuple-element.3) | data formatting | bytes 786432

commit v4 on v3

--- a/solution.py
+++ b/solution.py
@@ -93,6 +93,7 @@
     die_power,
     field,
     zx,
+    zu,
     zy,
     zz,
     diag,
@@ -116,6 +117,8 @@
     rough_side,
     rough_row,
     rough_corner,
+    rim,
+    rim_side,
     dies,
     fixed,
     all_dies,
@@ -192,6 +195,7 @@
         for at in (0, edge + 8):
             dies[n, :, pl.ds(at, 8), :] = jnp.zeros((slots, 8, edge), jnp.float32)
     rough_side[...] = jnp.zeros_like(rough_side)
+    rim_side[...] = jnp.zeros_like(rim_side)
     rough_row[...] = jnp.zeros_like(rough_row)
     rough_corner[...] = jnp.zeros_like(rough_corner)
     zx[:, :, 0:8, :] = jnp.zeros((layers, panes, 8, LANES), jnp.float32)
@@ -282,7 +286,9 @@
     def rough_copy(k, phase):
         dy, dx = DIRECTIONS[k]
         half = pl.ds(2 * phase, 2)
-        if dy == 0:
+        if dy == 0 and phase == 1:
+            src, dst = rim, rim_side.at[k - 2]
+        elif dy == 0:
             src = rough.at[half]
             dst = rough_side.at[k - 2, half]
         else:
@@ -322,10 +328,19 @@
     def line_ends(line, l, q):
         return shift(line, -(8 * l + 2 * q + 1), 1)
 
+    first_sub, last_sub = sub8 == 0, sub8 == 7
+
+    def row_above(u, l, p, r, x):
+        return shift(jnp.where(last_sub, u[l, p, pl.ds(r - 8, 8), :], x), 1, 0)
+
+    def row_below(u, l, p, r, x):
+        return shift(jnp.where(first_sub, u[l, p, pl.ds(r + 8, 8), :], x), -1, 0)
+
     early, late = TOP // 8 + 2, (height - TOP) // 8 - 1
 
     def across_down(r, l, p):
-        fx = inverse(field[l, p, pl.ds(r, 8), :] + field[l, p, pl.ds(r + 1, 8), :])
+        k = field[l, p, pl.ds(r, 8), :]
+        fx = inverse(k + row_below(field, l, p, r, k))
         zx[l, p, pl.ds(r, 8), :] = fx
         return fx
 
@@ -343,7 +358,9 @@
             for p in range(panes):
                 fy = fys[p]
                 zy[l, p, here, :] = fy
-                d = fxs[l][p] + zx[l, p, pl.ds(r - 1, 8), :] + fy + from_left(fys, p, ends)
+                fu = row_above(zx, l, p, r, fxs[l][p])
+                zu[l, p, here, :] = fu
+                d = fxs[l][p] + fu + fy + from_left(fys, p, ends)
                 d = d + (field[2 * layers, p, here, :] if l == 0 else below[p])
                 if l < layers - 1:
                     below[p] = inverse(k[p] + ks[l + 1][p])
@@ -568,8 +585,8 @@
         totals = []
         for p in range(panes):
             total = field[layers + l, p, here, :]
-            total = total + zx[l, p, here, :] * u[l, p, pl.ds(r + 1, 8), :]
-            total = total + zx[l, p, pl.ds(r - 1, 8), :] * u[l, p, pl.ds(r - 1, 8), :]
+            total = total + zx[l, p, here, :] * row_below(u, l, p, r, us[l][p])
+            total = total + zu[l, p, here, :] * row_above(u, l, p, r, us[l][p])
             total = total + fys[p] * from_right(us[l], p, ends) + from_left(flows, p, ends)
             if l > 0:
                 total = total + zz[l - 1, p, here, :] * us[l - 1][p]
@@ -619,9 +636,20 @@
             )
 
     gathered(layers, 2)
+    lane_r = iota((crows, LANES), 1) % ccols
+    rim[...] = jnp.where(
+        (lane_r < HALO) | (lane_r >= ccols - HALO),
+        rough[2],
+        jnp.where(lane_r < 2 * HALO, shift(rough[3], HALO, 1), shift(rough[3], -HALO, 1)),
+    )
     start_all(lambda k: rough_copy(k, 1), N_ROUGH)
 
     chigh = crows + 16
+
+    def side_of(n, phase, tile):
+        if phase == 0:
+            return rough_side[n, tile]
+        return shift(rim_side[n], (tile - 2) * (HALO if n else -HALO), 1)
 
     def join(phase):
         wait_all_recv(lambda k: rough_copy(k, phase), N_ROUGH)
@@ -641,7 +669,7 @@
                 )
 
             wide[target, 8 : 8 + crows, :] = joined(
-                rough_side[1, tile], rough[tile], rough_side[0, tile], crows
+                side_of(1, phase, tile), rough[tile], side_of(0, phase, tile), crows
             )
             wide[target, 0:8, :] = joined(
                 rough_corner[3, tile], rough_row[1, tile], rough_corner[2, tile], 8
@@ -725,7 +753,7 @@
     join(1)
     errors = [weights[l] * wide[layers + 1 + l] for l in range(layers)]
     top = top_w * top_rhs
-    for _ in range(NC - 1):
+    def next_errors(errors, top):
         new = []
         for l in range(layers):
             e = errors[l]
@@ -736,23 +764,45 @@
                 total = total + cz[l - 1] * errors[l - 1]
             total = total + (cz[l] * errors[l + 1] if l < layers - 1 else top_b * top)
             new.append((1.0 - RELAX) * e + weights[l] * total)
+        return new
+
+    def next_top(errors, top):
         nearby = (
             jnp.where(low_x, shift(top, 1, 0), 0.0)
             + jnp.where(high_x, shift(top, -1, 0), 0.0)
             + jnp.where(low_y, shift(top, 1, 1), 0.0)
             + jnp.where(high_y, shift(top, -1, 1), 0.0)
         )
-        top = top + top_w * (
+        return top + top_w * (
             top_rhs + top_b * errors[layers - 1] + top_c * nearby - top_d * top
         )
-        errors = new
+
+    for _ in range(NC - 2):
+        errors, top = next_errors(errors, top), next_top(errors, top)
+    last_top, top = top, next_top(errors, top)
+
     lane_c = iota((cell, LANES), 1)
     fix = jnp.zeros((cell, LANES), jnp.float32)
     for a in range(down):
         piece = shift(top[8 + a * cell : 8 + (a + 1) * cell], a * ccols - 8, 1)
         fix = jnp.where(lane_c // ccols == a, piece, fix)
-    all_fixes[me] = fix
+    row_f = iota((cell, LANES), 0)
+    blocks = down * across
+    short = all_fixes.shape[1]
+    rest = cell - short
+    stacks = short // rest if rest else 1
+
+    def stored(j):
+        return blocks + j // stacks, j % stacks
+
+    if rest:
+        for j in range(blocks):
+            at, stack = stored(j)
+            moved = shift(shift(fix, rest * stack - short, 0), cell * (at - j), 1)
+            fix = jnp.where((lane_c // cell == at) & (row_f // rest == stack), moved, fix)
+    all_fixes[me] = fix[:short]
     gather_start(1)
+    errors = next_errors(errors, last_top)
 
     pick = (iota((LANES, cols), 0) == 8 + iota((LANES, cols), 1) // RATIO).astype(jnp.float32)
     fine = two_part_dot(jnp.concatenate(errors, axis=0), pick)
@@ -804,7 +854,17 @@
         pr, pc = spot // span, lax.rem(spot, span)
         target = (pr // down) * tile_count + pc // across
         local = lax.rem(pr, down) * across + lax.rem(pc, across)
-        x = jnp.where(group == local, all_fixes[target], 0.0)
+        block = all_fixes[target]
+        if rest:
+            block = jnp.concatenate([block, jnp.zeros((rest, LANES), jnp.float32)], axis=0)
+            tail = jnp.where(
+                (group == blocks + local // stacks) & (row_f // rest == lax.rem(local, stacks)),
+                block, 0.0,
+            )
+            tail = sum(shift(tail, short - rest * n, 0) for n in range(stacks))
+            x = jnp.where(row_f < short, jnp.where(group == local, block, 0.0), tail)
+        else:
+            x = jnp.where(group == local, block, 0.0)
         step = LANES // 2
         while step >= cell:
             x = x + shift(x, step, 1)
@@ -862,6 +922,7 @@
             scratch(layers, rows, cols),
             scratch(slots, edge, edge),
             scratch(n_fields, panes, height, LANES),
+            scratch(*grid),
             scratch(*grid),
             scratch(*grid),
             scratch(layers - 1, panes, height, LANES),
@@ -886,10 +947,12 @@
             scratch(2, 4, crows, LANES),
             scratch(2, 4, 8, LANES),
             scratch(4, 4, 8, LANES),
+            scratch(crows, LANES),
+            scratch(2, crows, LANES),
             scratch(2, slots, edge + 16, edge),
             scratch(slots, cell, edge),
             scratch(count, cell + 8, LANES),
-            scratch(count, cell, LANES),
+            scratch(count, cell * cell * (rows // edge) * (cols // edge) // LANES, LANES),
             scratch(n_fields + 3, crows + 16, LANES),
             scratch(layers, panes, crows + 16, LANES),
             pltpu.SemaphoreType.DMA((len(DIRECTIONS) + 2 * N_ROUGH,)),

time: 42 us -> 40 us (0.952)
  Pallas kernels: 39 us -> 37 us
    pallas_call x1, Pallas kernels: 39 us -> 37 us  [per_device(): pl.pallas_call(functools.partial(kernel, grp_count, tile_count), out_shap...]
where the time goes in v4:
time: 40 us; the launch traced here: 39.8 us
  Pallas kernels  37 us (92%)
  local copies, waits for them, and re-layouts  2.15 us (5%)
  between operations  0.64 us (2%)
    pallas_call x1, Pallas kernels, per_device(): pl.pallas_call(functools.partial(kernel, grp_count, tile_count), out_shap...  37 us
    unnamed x2, local copies, waits for them, and re-layouts  2.15 us

profile of v4, /device:TPU:0, one launch (start us, length us, event | category | flops | bytes accessed | tf_op | source)
XLA Modules:
  0.0 39.8 jit_solution(14237736802088452918)
XLA Ops:
  0.6 37.0 %shard_map.95 = (f32[6,384,256]{2,1,0:T(8,128)S(1)}, f32[6,128,128]{2,1,0:T(8,128)S(1)}) custom-call(s32[6,384,256]{2,1,0:T(8,128)} %material_far.1, f32[8]{0:T(128)} %table.1, f32[384,256]{1,0:T(8,128)} %heat_sink_far.1, f32[6,384,256]{2,1,0:T(8,128)} %source_far.1, f32[6,128,128]{2,1,0:T(8,128)} %die_power_far.1, f32[6]{0:T(128)} %die_conduct.1, f32[6]{0:T(128)} %bond.1, ...), custom_call_target="tpu_custom_call" | custom-call | tf_op jit(solution)/shard_map/pallas_call | solution.py:911
  37.6 1.4 %copy.12 = f32[6,384,256]{2,1,0:T(8,128)} copy(f32[6,384,256]{2,1,0:T(8,128)S(1)} %get-tuple-element.2) | data formatting | bytes 4718592
  39.1 0.7 %copy.13 = f32[6,128,128]{2,1,0:T(8,128)} copy(f32[6,128,128]{2,1,0:T(8,128)S(1)} %get-tuple-element.3) | data formatting | bytes 786432

commit v5 on v4

--- a/solution.py
+++ b/solution.py
@@ -74,6 +74,32 @@
     )
 
 
+def die_diagonal(c, b, edge):
+    col, row = iota((8, edge), 1), iota((8, edge), 0)
+    inner = jnp.where(col > 0, 1.0, 0.0) + jnp.where(col < edge - 1, 1.0, 0.0) + 1.0
+    ds = [
+        c * (inner + jnp.where(row > 0, 1.0, 0.0)) + b,
+        c * (inner + 1.0) + b,
+        c * (inner + jnp.where(row < 7, 1.0, 0.0)) + b,
+    ]
+
+    def full(x):
+        return jnp.concatenate([x[0]] + [x[1]] * (edge // 8 - 2) + [x[2]], axis=0)
+
+    return full(ds), full([guarded_weight(d) for d in ds])
+
+
+def around(ref):
+    edge = ref.shape[1]
+    beside = jnp.abs(iota((edge, edge), 0) - iota((edge, edge), 1)) == 1
+    v = ref[pl.ds(8, edge), :]
+    return (
+        ref[pl.ds(7, edge), :]
+        + ref[pl.ds(9, edge), :]
+        + two_part_dot(v, beside.astype(jnp.float32))
+    )
+
+
 def kernel(
     grp_count,
     tile_count,
@@ -86,11 +112,12 @@
     bond,
     place,
     out,
-    die_out,
+    dies,
+    fixed,
+    die_power,
     material,
     heat_sink,
     source,
-    die_power,
     field,
     zx,
     zu,
@@ -119,8 +146,6 @@
     rough_corner,
     rim,
     rim_side,
-    dies,
-    fixed,
     all_dies,
     all_fixes,
     wide,
@@ -215,7 +240,11 @@
     def left_lane(f):
         return 64 + 8 * (f // 2) + HALO * (1 - f % 2)
 
-    doubled = [jnp.full((8, LANES), 2.0 * table[m], jnp.float32) for m in range(table.shape[0])]
+    kinds = table.shape[0]
+    doubled = [2.0 * table[m] for m in range(kinds)]
+    listed = jnp.zeros((8, LANES), jnp.float32)
+    for m in range(min(kinds, 8)):
+        listed = jnp.where(sub8 == m, doubled[m], listed)
 
     @pl.loop(0, pieces)
     def _(n):
@@ -233,17 +262,9 @@
                     part = slice(p * LANES, (p + 1) * LANES)
                     if f < layers:
                         kind = material[f, pl.ds(r, 8), part]
-                        values = list(doubled)
-                        bit = 1
-                        while len(values) > 1:
-                            odd = (kind & bit) != 0
-                            values = [
-                                jnp.where(odd, values[m + 1], values[m]) if m + 1 < len(values) else values[m]
-                                for m in range(0, len(values), 2)
-                            ]
-                            bit *= 2
-                        summed[p].append(values[0])
-                        x = inverse(values[0])
+                        k2 = jnp.take_along_axis(listed, kind, axis=0)
+                        summed[p].append(k2)
+                        x = inverse(k2)
                     elif f < 2 * layers:
                         x = source[f - layers, pl.ds(r, 8), part]
                     else:
@@ -385,29 +406,7 @@
 
     col_d = iota((8, LANES), 1)
     one, none = jnp.float32(1.0), jnp.float32(0.0)
-    inner = jnp.where(col_d > 0, one, none) + jnp.where(col_d < edge - 1, one, none) + 1.0
-    first_row = jnp.where(sub8 > 0, one, none)
-    last_row = jnp.where(sub8 < 7, one, none)
-    beside = (
-        jnp.abs(iota((edge, edge), 0) - iota((edge, edge), 1)) == 1
-    ).astype(jnp.float32)
     body = pl.ds(8, edge)
-    tall = edge // 8
-
-    def die_diagonal(c, b):
-        tops = [c * (inner + first_row) + b, c * (inner + 1.0) + b, c * (inner + last_row) + b]
-        ws = [guarded_weight(d) for d in tops]
-
-        def full(x):
-            return jnp.concatenate([x[0]] + [x[1]] * (tall - 2) + [x[2]], axis=0)
-
-        return full(tops), full(ws)
-
-    def around(n, s):
-        v = dies[n, s, body, :]
-        return (
-            dies[n, s, pl.ds(7, edge), :] + dies[n, s, pl.ds(9, edge), :] + two_part_dot(v, beside)
-        )
 
     rows_in = (iota((cell, edge), 0) == iota((cell, edge), 1) // RATIO).astype(jnp.bfloat16)
     rows_in = jnp.concatenate([rows_in, rows_in], axis=1)
@@ -418,10 +417,10 @@
         c, b = die_conduct[s], bond[s]
         live = jnp.where(place[s] >= 0, 1.0, 0.0)
         p = die_power[s]
-        d, wt = die_diagonal(c, b)
+        d, wt = die_diagonal(c, b, edge)
         dies[0, s, body, :] = wt * p
-        dies[1, s, body, :] = (1.0 - RELAX) * dies[0, s, body, :] + wt * (p + c * around(0, s))
-        resid = p + c * around(1, s) - d * dies[1, s, body, :]
+        dies[1, s, body, :] = (1.0 - RELAX) * dies[0, s, body, :] + wt * (p + c * around(dies.at[0, s]))
+        resid = p + c * around(dies.at[1, s]) - d * dies[1, s, body, :]
         cols_in = (
             iota((edge, LANES), 0) // RATIO + cell * s == iota((edge, LANES), 1)
         ).astype(jnp.float32)
@@ -869,20 +868,8 @@
         while step >= cell:
             x = x + shift(x, step, 1)
             step //= 2
-        c, b = die_conduct[s], bond[s]
         live = jnp.where(place[s] >= 0, 1.0, 0.0)
-        p = die_power[s]
-        wt = die_diagonal(c, b)[1]
         fixed[s] = live * two_part_dot(x, cols_out)
-        for k in range(tall):
-            dies[0, s, pl.ds(8 + 8 * k, 8), :] = (
-                dies[1, s, pl.ds(8 + 8 * k, 8), :] + fixed[s, pl.ds(k, 1), :]
-            )
-        for n in range(NU):
-            v = (1.0 - RELAX) * dies[n % 2, s, body, :] + wt * (p + c * around(n % 2, s))
-            if n < NU - 1:
-                dies[(n + 1) % 2, s, body, :] = v
-        die_out[s] = live * v
 
     wait_all_send(halo_copy, len(DIRECTIONS))
     for phase in range(2):
@@ -908,19 +895,20 @@
         return pltpu.VMEM(shape, f32)
 
     grid = (layers, panes, height, LANES)
-    return pl.pallas_call(
+    heats = pl.pallas_call(
         functools.partial(kernel, grp_count, tile_count),
         out_shape=(
             pltpu.VMEM((layers, rows, cols), f32),
+            pltpu.VMEM((2, slots, edge + 16, edge), f32),
+            pltpu.VMEM((slots, cell, edge), f32),
             pltpu.VMEM((slots, edge, edge), f32),
         ),
         in_specs=[far, smem, far, far, far, smem, smem, smem],
-        out_specs=(vmem, vmem),
+        out_specs=(vmem,) * 4,
         scratch_shapes=[
             pltpu.VMEM(material.shape, material.dtype),
             scratch(rows, cols),
             scratch(layers, rows, cols),
-            scratch(slots, edge, edge),
             scratch(n_fields, panes, height, LANES),
             scratch(*grid),
             scratch(*grid),
@@ -949,8 +937,6 @@
             scratch(4, 4, 8, LANES),
             scratch(crows, LANES),
             scratch(2, crows, LANES),
-            scratch(2, slots, edge + 16, edge),
-            scratch(slots, cell, edge),
             scratch(count, cell + 8, LANES),
             scratch(count, cell * cell * (rows // edge) * (cols // edge) // LANES, LANES),
             scratch(n_fields + 3, crows + 16, LANES),
@@ -966,6 +952,66 @@
             collective_id=0, has_side_effects=True, vmem_limit_bytes=60 * 1024 * 1024
         ),
     )(*args)
+
+    return finish_dies(*heats, args[5], args[6], args[7])
+
+
+def finish_kernel(
+    heat, dies, fixed, die_power, die_conduct, bond, place, heat_out, die_out, work, done,
+    heat_sem, die_sem,
+):
+    slots, edge, _ = die_power.shape
+    body = pl.ds(8, edge)
+    move = pltpu.make_async_copy(heat, heat_out, heat_sem)
+    move.start()
+    moves = []
+    for at in (0, edge + 8):
+        work[:, :, pl.ds(at, 8), :] = jnp.zeros((2, slots, 8, edge), jnp.float32)
+    for s in range(slots):
+        c, b = die_conduct[s], bond[s]
+        live = jnp.where(place[s] >= 0, 1.0, 0.0)
+        p = die_power[s]
+        wt = die_diagonal(c, b, edge)[1]
+        for k in range(edge // 8):
+            work[0, s, pl.ds(8 + 8 * k, 8), :] = (
+                dies[1, s, pl.ds(8 + 8 * k, 8), :] + fixed[s, pl.ds(k, 1), :]
+            )
+        for n in range(NU):
+            now = work.at[n % 2, s]
+            v = (1.0 - RELAX) * now[body, :] + wt * (p + c * around(now))
+            if n < NU - 1:
+                work[(n + 1) % 2, s, body, :] = v
+        done[s] = live * v
+    for s in range(slots):
+        moves.append(pltpu.make_async_copy(done.at[s], die_out.at[s], die_sem.at[s]))
+        moves[-1].start()
+    for each in moves:
+        each.wait()
+    move.wait()
+
+
+def finish_dies(heat, dies, fixed, die_power, *params):
+    slots, edge, _ = die_power.shape
+    near = [pltpu.with_memory_space_constraint(x, pltpu.VMEM) for x in (dies, fixed, die_power)]
+    anywhere = pl.BlockSpec(memory_space=pl.ANY)
+    vmem = pl.BlockSpec(memory_space=pltpu.VMEM)
+    smem = pl.BlockSpec(memory_space=pltpu.SMEM)
+    return pl.pallas_call(
+        finish_kernel,
+        out_shape=(
+            jax.ShapeDtypeStruct(heat.shape, heat.dtype),
+            jax.ShapeDtypeStruct(die_power.shape, die_power.dtype),
+        ),
+        in_specs=[anywhere] + [vmem] * 3 + [smem] * 3,
+        out_specs=(anywhere, anywhere),
+        scratch_shapes=[
+            pltpu.VMEM(dies.shape, jnp.float32),
+            pltpu.VMEM(die_power.shape, jnp.float32),
+            pltpu.SemaphoreType.DMA,
+            pltpu.SemaphoreType.DMA((slots,)),
+        ],
+        compiler_params=pltpu.CompilerParams(vmem_limit_bytes=8 * 1024 * 1024),
+    )(heat, *near, *params)
 
 
 def solution(mesh):

time: 40 us -> 38.7 us (0.968)
  local copies, waits for them, and re-layouts: 2.15 us -> 0.01 us
  Pallas kernels: 37 us -> 37.8 us
    unnamed x2 -> x6, local copies, waits for them, and re-layouts: 2.15 us -> 0.01 us
    pallas_call x0 -> x1, Pallas kernels: none -> 2.14 us  [finish_dies(): pl.pallas_call(finish_kernel, out_shape=(jax.ShapeDtypeStruct(heat.shape,...]
    pallas_call x1, Pallas kernels: 37 us -> 35.7 us  [per_device(): pl.pallas_call(functools.partial(kernel, grp_count, tile_count), out_shap...]
where the time goes in v5:
time: 38.7 us; the launch traced here: 38.5 us
  Pallas kernels  37.8 us (98%)
  between operations  0.69 us (2%)
    pallas_call x1, Pallas kernels, per_device(): pl.pallas_call(functools.partial(kernel, grp_count, tile_count), out_shap...  35.7 us
    pallas_call x1, Pallas kernels, finish_dies(): pl.pallas_call(finish_kernel, out_shape=(jax.ShapeDtypeStruct(heat.shape,...  2.14 us

profile of v5, /device:TPU:0, one launch (start us, length us, event | category | flops | bytes accessed | tf_op | source)
XLA Modules:
  0.0 38.5 jit_solution(159139595483169067)
XLA Ops:
  0.6 0.0 copy-start.2
  0.6 0.0 copy-start.1
  0.7 0.0 copy-start
  0.7 35.7 %shard_map.95 = (f32[6,384,256]{2,1,0:T(8,128)S(1)}, f32[2,6,144,128]{3,2,1,0:T(8,128)S(1)}, f32[6,16,128]{2,1,0:T(8,128)S(1)}, f32[6,128,128]{2,1,0:T(8,128)S(1)}) custom-call(s32[6,384,256]{2,1,0:T(8,128)} %material_far.1, f32[8]{0:T(128)} %table.1, f32[384,256]{1,0:T(8,128)} %heat_sink_far.1, f32[6,384,256]{2,1,0:T(8,128)} %source_far.1, ...), custom_call_target="tpu_custom_call" | custom-call | tf_op jit(solution)/shard_map/pallas_call | solution.py:898
  36.3 0.0 copy-done.2
  36.4 0.0 copy-done.1
  36.4 0.0 copy-done
  36.4 2.1 %shard_map.96 = (f32[6,384,256]{2,1,0:T(8,128)}, f32[6,128,128]{2,1,0:T(8,128)}) custom-call(f32[6,384,256]{2,1,0:T(8,128)S(1)} %get-tuple-element.6.heat, f32[2,6,144,128]{3,2,1,0:T(8,128)S(1)} %get-tuple-element.7.dies, f32[6,16,128]{2,1,0:T(8,128)S(1)} %get-tuple-element.8.fixed, f32[6,128,128]{2,1,0:T(8,128)S(1)} %get-tuple-element.9.die_power, ...), custom_call_target="tpu_custom_call" | custom-call | tf_op jit(solution)/shard_map/pallas_call | solution.py:999
Async XLA Ops:
  0.6 35.7 %copy-start.2 = (s32[6]{0:T(128)S(1)}, s32[6]{0:T(128)}, u32[]{:S(2)}) copy-start(s32[6]{0:T(128)} %place.3) | copy-start | bytes 76
  0.6 35.7 %copy-start.1 = (f32[6]{0:T(128)S(1)}, f32[6]{0:T(128)}, u32[]{:S(2)}) copy-start(f32[6]{0:T(128)} %bond.3) | copy-start | bytes 76
  0.7 35.7 %copy-start = (f32[6]{0:T(128)S(1)}, f32[6]{0:T(128)}, u32[]{:S(2)}) copy-start(f32[6]{0:T(128)} %die_conduct.3) | copy-start | bytes 76

commit v6 on v5

--- a/solution.py
+++ b/solution.py
@@ -15,7 +15,7 @@
 LANES = 128
 FAR = 1e30
 TINY = 1e-25
-UNROLL = 5
+UNROLL = 6
 MESH = pl.DeviceIdType.MESH
 DIRECTIONS = ((-1, 0), (1, 0), (0, -1), (0, 1), (-1, -1), (-1, 1), (1, -1), (1, 1), (-1, 0), (1, 0))
 N_ROUGH = 8
@@ -234,12 +234,6 @@
     lane8 = iota((8, LANES), 1)
     sub8 = iota((8, LANES), 0)
 
-    def right_lane(f):
-        return HALO * f
-
-    def left_lane(f):
-        return 64 + 8 * (f // 2) + HALO * (1 - f % 2)
-
     kinds = table.shape[0]
     doubled = [2.0 * table[m] for m in range(kinds)]
     listed = jnp.zeros((8, LANES), jnp.float32)
@@ -254,7 +248,7 @@
         @pl.loop(0, piece // 8, unroll=unroll_of(piece // 8, 4))
         def _(i):
             r = pl.multiple_of(n * piece + i * 8, 8)
-            edges = jnp.zeros((8, LANES), jnp.float32)
+            kept = [jnp.zeros((8, LANES), jnp.float32)] * 2
             summed = [[] for _ in range(panes)]
             for f in range(n_fields):
                 xs = []
@@ -272,11 +266,15 @@
                         summed[p].append(x)
                     field[f, p, pl.ds(TOP + r, 8), :] = x
                     xs.append(x)
-                a, b = right_lane(f), left_lane(f)
-                right = shift(xs[-1], HALO + a, 1)
-                left = shift(xs[0], b, 1)
-                edges = jnp.where((lane8 >= a) & (lane8 < a + HALO), right, edges)
-                edges = jnp.where((lane8 >= b) & (lane8 < b + HALO), left, edges)
+                at = 8 * (f // 2) + HALO * (f % 2)
+                both = shift(jnp.where(lane8 < HALO, xs[0], xs[-1]), HALO + at, 1)
+                kept[f % 2] = jnp.where((lane8 >= at) & (lane8 < at + 8), both, kept[f % 2])
+            even, odd = kept
+            edges = jnp.where(
+                lane8 < 64,
+                jnp.where(lane8 % 8 < HALO, even, odd),
+                jnp.where(lane8 % 8 < HALO, shift(odd, 56, 1), shift(even, 64, 1)),
+            )
             packed[pl.ds(r, 8), :] = edges
             for p in range(panes):
                 sums[pl.ds(r, 8), p * LANES : (p + 1) * LANES] = row_sums(summed[p])
@@ -845,14 +843,21 @@
 
     sweep(ua, finish, TOP // 8, (height - TOP) // 8, 1, 1)
 
-    gather_wait(1)
-    group = lane_c // cell
-    cols_out = (iota((LANES, edge), 0) == iota((LANES, edge), 1) // RATIO).astype(jnp.float32)
+    wait_all_send(halo_copy, len(DIRECTIONS))
+    for phase in range(2):
+        wait_all_send(lambda k: rough_copy(k, phase), N_ROUGH)
+    homes = []
     for s in range(slots):
         spot = jnp.maximum(place[s], 0)
         pr, pc = spot // span, lax.rem(spot, span)
         target = (pr // down) * tile_count + pc // across
         local = lax.rem(pr, down) * across + lax.rem(pc, across)
+        homes.append((target, local))
+    gather_wait(1)
+    group = lane_c // cell
+    cols_out = (iota((LANES, edge), 0) == iota((LANES, edge), 1) // RATIO).astype(jnp.float32)
+    for s in range(slots):
+        target, local = homes[s]
         block = all_fixes[target]
         if rest:
             block = jnp.concatenate([block, jnp.zeros((rest, LANES), jnp.float32)], axis=0)
@@ -870,10 +875,6 @@
             step //= 2
         live = jnp.where(place[s] >= 0, 1.0, 0.0)
         fixed[s] = live * two_part_dot(x, cols_out)
-
-    wait_all_send(halo_copy, len(DIRECTIONS))
-    for phase in range(2):
-        wait_all_send(lambda k: rough_copy(k, phase), N_ROUGH)
 
 
 def per_device(grp_count, tile_count, *args):

time: 38.7 us -> 38.6 us (level)
  no operation moved by 1% of the time
where the time goes in v6:
time: 38.6 us; the launch traced here: 38.5 us
  Pallas kernels  37.8 us (98%)
  between operations  0.69 us (2%)
    pallas_call x1, Pallas kernels, per_device(): pl.pallas_call(functools.partial(kernel, grp_count, tile_count), out_shap...  35.6 us
    pallas_call x1, Pallas kernels, finish_dies(): pl.pallas_call(finish_kernel, out_shape=(jax.ShapeDtypeStruct(heat.shape,...  2.14 us

profile of v6, /device:TPU:0, one launch (start us, length us, event | category | flops | bytes accessed | tf_op | source)
XLA Modules:
  0.0 38.5 jit_solution(2416138522780374071)
XLA Ops:
  0.6 0.0 copy-start.2
  0.6 0.0 copy-start.1
  0.7 0.0 copy-start
  0.7 35.6 %shard_map.95 = (f32[6,384,256]{2,1,0:T(8,128)S(1)}, f32[2,6,144,128]{3,2,1,0:T(8,128)S(1)}, f32[6,16,128]{2,1,0:T(8,128)S(1)}, f32[6,128,128]{2,1,0:T(8,128)S(1)}) custom-call(s32[6,384,256]{2,1,0:T(8,128)} %material_far.1, f32[8]{0:T(128)} %table.1, f32[384,256]{1,0:T(8,128)} %heat_sink_far.1, f32[6,384,256]{2,1,0:T(8,128)} %source_far.1, ...), custom_call_target="tpu_custom_call" | custom-call | tf_op jit(solution)/shard_map/pallas_call | solution.py:899
  36.3 0.0 copy-done.2
  36.3 0.0 copy-done.1
  36.3 0.0 copy-done
  36.3 2.1 %shard_map.96 = (f32[6,384,256]{2,1,0:T(8,128)}, f32[6,128,128]{2,1,0:T(8,128)}) custom-call(f32[6,384,256]{2,1,0:T(8,128)S(1)} %get-tuple-element.6.heat, f32[2,6,144,128]{3,2,1,0:T(8,128)S(1)} %get-tuple-element.7.dies, f32[6,16,128]{2,1,0:T(8,128)S(1)} %get-tuple-element.8.fixed, f32[6,128,128]{2,1,0:T(8,128)S(1)} %get-tuple-element.9.die_power, ...), custom_call_target="tpu_custom_call" | custom-call | tf_op jit(solution)/shard_map/pallas_call | solution.py:1000
Async XLA Ops:
  0.6 35.7 %copy-start.2 = (s32[6]{0:T(128)S(1)}, s32[6]{0:T(128)}, u32[]{:S(2)}) copy-start(s32[6]{0:T(128)} %place.3) | copy-start | bytes 76
  0.6 35.7 %copy-start.1 = (f32[6]{0:T(128)S(1)}, f32[6]{0:T(128)}, u32[]{:S(2)}) copy-start(f32[6]{0:T(128)} %bond.3) | copy-start | bytes 76
  0.7 35.7 %copy-start = (f32[6]{0:T(128)S(1)}, f32[6]{0:T(128)}, u32[]{:S(2)}) copy-start(f32[6]{0:T(128)} %die_conduct.3) | copy-start | bytes 76

commit v7 on v6

--- a/solution.py
+++ b/solution.py
@@ -983,9 +983,12 @@
             if n < NU - 1:
                 work[(n + 1) % 2, s, body, :] = v
         done[s] = live * v
-    for s in range(slots):
-        moves.append(pltpu.make_async_copy(done.at[s], die_out.at[s], die_sem.at[s]))
-        moves[-1].start()
+        if s in (slots // 2 - 1, slots - 1):
+            for ready in range(len(moves), s + 1):
+                moves.append(
+                    pltpu.make_async_copy(done.at[ready], die_out.at[ready], die_sem.at[ready])
+                )
+                moves[-1].start()
     for each in moves:
         each.wait()
     move.wait()

time: 38.6 us -> 38.8 us (level)
  no operation moved by 1% of the time
where the time goes in v7:
time: 38.8 us; the launch traced here: 38.6 us
  Pallas kernels  37.9 us (98%)
  between operations  0.69 us (2%)
    pallas_call x1, Pallas kernels, per_device(): pl.pallas_call(functools.partial(kernel, grp_count, tile_count), out_shap...  35.6 us
    pallas_call x1, Pallas kernels, finish_dies(): pl.pallas_call(finish_kernel, out_shape=(jax.ShapeDtypeStruct(heat.shape,...  2.29 us

profile of v7, /device:TPU:0, one launch (start us, length us, event | category | flops | bytes accessed | tf_op | source)
XLA Modules:
  0.0 38.6 jit_solution(15077614575539332610)
XLA Ops:
  0.6 0.0 copy-start.2
  0.6 0.0 copy-start.1
  0.7 0.0 copy-start
  0.7 35.6 %shard_map.95 = (f32[6,384,256]{2,1,0:T(8,128)S(1)}, f32[2,6,144,128]{3,2,1,0:T(8,128)S(1)}, f32[6,16,128]{2,1,0:T(8,128)S(1)}, f32[6,128,128]{2,1,0:T(8,128)S(1)}) custom-call(s32[6,384,256]{2,1,0:T(8,128)} %material_far.1, f32[8]{0:T(128)} %table.1, f32[384,256]{1,0:T(8,128)} %heat_sink_far.1, f32[6,384,256]{2,1,0:T(8,128)} %source_far.1, ...), custom_call_target="tpu_custom_call" | custom-call | tf_op jit(solution)/shard_map/pallas_call | solution.py:899
  36.3 0.0 copy-done.2
  36.3 0.0 copy-done.1
  36.3 0.0 copy-done
  36.3 2.3 %shard_map.96 = (f32[6,384,256]{2,1,0:T(8,128)}, f32[6,128,128]{2,1,0:T(8,128)}) custom-call(f32[6,384,256]{2,1,0:T(8,128)S(1)} %get-tuple-element.6.heat, f32[2,6,144,128]{3,2,1,0:T(8,128)S(1)} %get-tuple-element.7.dies, f32[6,16,128]{2,1,0:T(8,128)S(1)} %get-tuple-element.8.fixed, f32[6,128,128]{2,1,0:T(8,128)S(1)} %get-tuple-element.9.die_power, ...), custom_call_target="tpu_custom_call" | custom-call | tf_op jit(solution)/shard_map/pallas_call | solution.py:1003
Async XLA Ops:
  0.6 35.7 %copy-start.2 = (s32[6]{0:T(128)S(1)}, s32[6]{0:T(128)}, u32[]{:S(2)}) copy-start(s32[6]{0:T(128)} %place.3) | copy-start | bytes 76
  0.6 35.7 %copy-start.1 = (f32[6]{0:T(128)S(1)}, f32[6]{0:T(128)}, u32[]{:S(2)}) copy-start(f32[6]{0:T(128)} %bond.3) | copy-start | bytes 76
  0.7 35.7 %copy-start = (f32[6]{0:T(128)S(1)}, f32[6]{0:T(128)}, u32[]{:S(2)}) copy-start(f32[6]{0:T(128)} %die_conduct.3) | copy-start | bytes 76
